TPU v7x, 128 devices: a whole 4x4x4 slice. The times are simulated.
128 devices in a mesh: dp: 8 (over x_lo, z), tensor: 16 (over x_hi, y, core).
Axes of the slice: x: 4 (x_hi: 2, x_lo: 2; x = x_hi * 2 + x_lo), y: 4, z: 4, core: 2. Of those that a mesh axis runs over, the one named last changes fastest.
Arguments:
- layer_input: bfloat16 [1024, 5376], P('tensor', 'dp'), may hold values from -6 to 6
- gate_weight: bfloat16 [5376, 21504], P('dp', 'tensor'), may hold values from -0.078125 to 0.078125
- up_weight: bfloat16 [5376, 21504], P('dp', 'tensor'), may hold values from -0.078125 to 0.078125
- down_weight: bfloat16 [21504, 5376], P('tensor', 'dp'), may hold values from -0.0390625 to 0.0390625
- granularity: int32 [16], replicated, may hold values from 0 to 3, as said below
- out_grad: bfloat16 [1024, 5376], P('tensor', 'dp'), may hold values from -4 to 4
Outputs:
- layer_output: bfloat16 [1024, 5376], P('tensor', 'dp')
- input_grad: bfloat16 [1024, 5376], P('tensor', 'dp')
- gate_grad: bfloat16 [5376, 21504], P('dp', 'tensor')
- up_grad: bfloat16 [5376, 21504], P('dp', 'tensor')
- down_grad: bfloat16 [21504, 5376], P('tensor', 'dp')
Inputs may be any that keep to these rules, and one draw needn't show every extreme that they name: `granularity`: the nested level of each sequence; in every draw some sequence has level 0 and some has level 3.
All inputs are finite; a program needn't handle non-finite values.
Results may differ from a plain program's by a relative error of at most 0.0051.
Values may be sent and summed in bfloat16 or wider, within the bound.
A program may use at most 128 MiB of HBM per device.

v0:
```python
import jax
import jax.numpy as jnp
from jax import lax
from jax.sharding import PartitionSpec as P

FF = 21504
LEN = 64


def contract(left, right, left_dim, right_dim):
    return lax.dot_general(
        left, right, (((left_dim,), (right_dim,)), ((), ())), preferred_element_type=jnp.float32
    )


def rows_term(arrays, product):

    def term(first_row, row_count):
        pieces = tuple(
            (lax.dynamic_slice_in_dim(array, first_row, row_count, 0) for array in arrays)
        )
        return product(pieces)

    return term


def activate(gate_up, widths, first_seq, col_first, hidden_cols):
    seq_count = gate_up.shape[0] // LEN
    row_width = jnp.repeat(
        lax.dynamic_slice_in_dim(widths, first_seq, seq_count, 0),
        LEN,
        total_repeat_length=seq_count * LEN,
    )
    col_index = col_first + jnp.arange(hidden_cols, dtype=jnp.int32)
    col_mask = (col_index[None, :] < row_width[:, None]).astype(jnp.float32)
    gate_pre = gate_up[:, :hidden_cols]
    up_pre = gate_up[:, hidden_cols:]
    gate_sig = jax.nn.sigmoid(gate_pre)
    gate_act = gate_pre * gate_sig
    hidden = (gate_act * up_pre * col_mask).astype(jnp.bfloat16)
    return (hidden, (gate_pre, up_pre, gate_sig, gate_act, col_mask))


def backprop(hidden_grad, stored):
    gate_pre, up_pre, gate_sig, gate_act, col_mask = stored
    gate_delta = (
        hidden_grad * up_pre * gate_sig * (1.0 + gate_pre * (1.0 - gate_sig)) * col_mask
    ).astype(jnp.bfloat16)
    up_delta = (hidden_grad * gate_act * col_mask).astype(jnp.bfloat16)
    return (gate_delta, up_delta)


def finish(term, tokens):
    return lax.psum_scatter(
        term(jnp.int32(0), tokens // lax.axis_size("tensor") * lax.axis_size("tensor")),
        "tensor",
        scatter_dimension=0,
        tiled=True,
    ).astype(jnp.bfloat16)


def local(layer_input, gate_weight, up_weight, down_weight, granularity, out_grad):
    hidden_cols = gate_weight.shape[1]
    tensor_index = lax.axis_index("tensor")
    data_index = lax.axis_index("dp")
    col_first = tensor_index * hidden_cols
    widths = jnp.left_shift(jnp.int32(FF // 8), granularity)
    input_all, grad_all = (
        lax.all_gather(layer_input, "tensor", axis=0, tiled=True),
        lax.all_gather(out_grad, "tensor", axis=0, tiled=True),
    )
    tokens = input_all.shape[0]
    tok_dev = tokens // lax.axis_size("dp")
    seq_dev = tok_dev // LEN

    def gate_product(segment):
        return jnp.concatenate(
            [contract(segment[0], gate_weight, 1, 0), contract(segment[0], up_weight, 1, 0)], 1
        )

    gate_term = rows_term((input_all,), gate_product)

    def back_product(segment):
        return contract(segment[0], down_weight, 1, 1)

    back_term = rows_term((grad_all,), back_product)
    gate_up = lax.psum_scatter(
        gate_term(jnp.int32(0), tok_dev * lax.axis_size("dp")),
        "dp",
        scatter_dimension=0,
        tiled=True,
    )
    hidden, stored = activate(gate_up, widths, data_index * seq_dev, col_first, hidden_cols)
    hidden_all = lax.all_gather(hidden, "dp", axis=0, tiled=True)

    def down_product(segment):
        return contract(segment[0], down_weight, 1, 0)

    layer_output = finish(rows_term((hidden_all,), down_product), tokens)
    hidden_grad = lax.psum_scatter(
        back_term(jnp.int32(0), tok_dev * lax.axis_size("dp")),
        "dp",
        scatter_dimension=0,
        tiled=True,
    )
    gate_delta, up_delta = backprop(hidden_grad, stored)
    gate_all, up_all = (
        lax.all_gather(gate_delta, "dp", axis=0, tiled=True),
        lax.all_gather(up_delta, "dp", axis=0, tiled=True),
    )

    def input_product(segment):
        return contract(segment[0], gate_weight, 1, 1) + contract(segment[1], up_weight, 1, 1)

    input_grad = finish(rows_term((gate_all, up_all), input_product), tokens)
    down_grad = contract(hidden_all, grad_all, 0, 0).astype(jnp.bfloat16)
    gate_grad = contract(input_all, gate_all, 0, 0).astype(jnp.bfloat16)
    up_grad = contract(input_all, up_all, 0, 0).astype(jnp.bfloat16)
    return (layer_output, input_grad, gate_grad, up_grad, down_grad)


def solution(mesh):
    in_specs = (
        P("tensor", "dp"),
        P("dp", "tensor"),
        P("dp", "tensor"),
        P("tensor", "dp"),
        P(),
        P("tensor", "dp"),
    )
    out_specs = (
        P("tensor", "dp"),
        P("tensor", "dp"),
        P("dp", "tensor"),
        P("dp", "tensor"),
        P("tensor", "dp"),
    )
    return jax.shard_map(local, mesh=mesh, in_specs=in_specs, out_specs=out_specs, check_vma=False)
```

profile of v0, /device:TPU:0, one launch (start us, length us, event | category | flops | bytes accessed | tf_op | source)
XLA Modules:
  0.0 616.5 jit_solution(18044599373373278689)
XLA Ops:
  8.0 0.7 all-gather.6.cloned.1.call-update
  8.7 50.4 %all-gather.10.cloned.1.call-done = bf16[1024,672]{1,0:T(8,128)(2,1)} async-done(((bf16[64,672]{1,0:T(8,128)(2,1)}), bf16[1024,672]{1,0:T(8,128)(2,1)}) %all-gather.10.cloned.1.call-update) | async-done | bytes 1376272 | tf_op jit(solution)/shard_map/all_gather | solution.py:70
  59.1 6.7 %fusion.10 = f32[1024,1344]{0,1:T(8,128)} fusion(bf16[1024,672]{1,0:T(8,128)(2,1)} %all-gather.10.cloned.1.call-done, bf16[1344,672]{0,1:T(8,128)(2,1)} %param.11), kind=kOutput, calls=%fused_computation.22 | convolution fusion | flops 1849688064 | bytes 8687616 | tf_op jit(solution)/shard_map/dot_general | solution.py:11
  65.9 40.7 %all-gather.6.cloned.1.call-done = bf16[1024,672]{1,0:T(8,128)(2,1)} async-done(((bf16[64,672]{1,0:T(8,128)(2,1)}), bf16[1024,672]{1,0:T(8,128)(2,1)}) %all-gather.6.cloned.1.call-update) | async-done | bytes 1376272 | tf_op jit(solution)/shard_map/all_gather | solution.py:69
  106.6 6.3 %fusion.7 = f32[1024,1344]{0,1:T(8,128)} fusion(bf16[1024,672]{1,0:T(8,128)(2,1)} %all-gather.6.cloned.1.call-done, bf16[672,1344]{1,0:T(8,128)(2,1)S(1)} %copy-done), kind=kOutput, calls=%fused_computation.19 | convolution fusion | flops 1849688064 | bytes 8687616 | tf_op jit(solution)/shard_map/dot_general | solution.py:11
  113.0 4.9 fusion.8
  117.8 10.7 %pad_maximum_fusion = f32[1024,2688]{0,1:T(8,128)} fusion(f32[1024,1344]{0,1:T(8,128)} %fusion.8, f32[1024,1344]{0,1:T(8,128)} %fusion.7), kind=kLoop, calls=%fused_computation | loop fusion | flops 2752512 | bytes 22020096 | tf_op jit(solution)/shard_map/concatenate | solution.py:77
  129.9 1.3 broadcast_select_fusion
  131.2 42.4 %reduce-scatter.9.cloned.1.call-done = f32[128,1344]{0,1:T(8,128)} async-done(((f32[1024,1344]{0,1:T(8,128)}), f32[128,1344]{0,1:T(8,128)}) %reduce-scatter.9.cloned.1.call-update) | async-done | bytes 688144 | tf_op jit(solution)/shard_map/reduce_scatter | solution.py:100
  173.6 118.6 %reduce-scatter.5.cloned.1.call-done = f32[128,2688]{0,1:T(8,128)} async-done(((f32[1024,2688]{0,1:T(8,128)}), f32[128,2688]{0,1:T(8,128)}) %reduce-scatter.5.cloned.1.call-update) | async-done | bytes 1376272 | tf_op jit(solution)/shard_map/reduce_scatter | solution.py:87
  292.2 3.0 fusion.4
  296.7 46.9 %all-gather.12.cloned.1.call-done = bf16[1024,1344]{0,1:T(8,128)(2,1)} async-done(((bf16[128,1344]{0,1:T(8,128)(2,1)}), bf16[1024,1344]{0,1:T(8,128)(2,1)}) %all-gather.12.cloned.1.call-update) | async-done | bytes 2752528 | tf_op jit(solution)/shard_map/all_gather | solution.py:108
  343.6 6.1 fusion.11
  349.8 46.8 %all-gather.14.cloned.1.call-done = bf16[1024,1344]{0,1:T(8,128)(2,1)} async-done(((bf16[128,1344]{0,1:T(8,128)(2,1)}), bf16[1024,1344]{0,1:T(8,128)(2,1)}) %all-gather.14.cloned.1.call-update) | async-done | bytes 2752528 | tf_op jit(solution)/shard_map/all_gather | solution.py:109
  396.5 7.6 %convolution_add_fusion = f32[1024,672]{1,0:T(8,128)} fusion(f32[1024,672]{1,0:T(8,128)} %fusion.11, bf16[1024,1344]{0,1:T(8,128)(2,1)} %all-gather.14.cloned.1.call-done, bf16[672,1344]{1,0:T(8,128)(2,1)} %param.10), kind=kOutput, calls=%fused_computation.6 | convolution fusion | flops 1850376192 | bytes 10063872 | tf_op jit(solution)/shard_map/dot_general | solution.py:11
  404.3 45.3 %all-gather.8.cloned.1.call-done = bf16[1024,1344]{0,1:T(8,128)(2,1)} async-done(((bf16[128,1344]{0,1:T(8,128)(2,1)}), bf16[1024,1344]{0,1:T(8,128)(2,1)}) %all-gather.8.cloned.1.call-update) | async-done | bytes 2752528 | tf_op jit(solution)/shard_map/all_gather | solution.py:94
  449.6 6.6 %fusion.9 = f32[1024,672]{1,0:T(8,128)} fusion(bf16[1024,1344]{0,1:T(8,128)(2,1)} %all-gather.8.cloned.1.call-done, bf16[1344,672]{0,1:T(8,128)(2,1)} %param.11), kind=kOutput, calls=%fused_computation.21 | convolution fusion | flops 1849688064 | bytes 7311360 | tf_op jit(solution)/shard_map/dot_general | solution.py:11
  456.3 5.6 fusion
  461.9 3.7 fusion.1
  465.5 3.7 convolution_convert_fusion
  469.2 61.0 %reduce-scatter.11.cloned.1.call-done = f32[64,672]{1,0:T(8,128)} async-done(((f32[1024,672]{1,0:T(8,128)}), f32[64,672]{1,0:T(8,128)}) %reduce-scatter.11.cloned.1.call-update) | async-done | bytes 172048 | tf_op jit(solution)/shard_map/reduce_scatter | solution.py:54
  530.2 1.6 convert_element_type.35
  531.8 76.6 %reduce-scatter.7.cloned.1.call-done = f32[64,672]{1,0:T(8,128)} async-done(((f32[1024,672]{1,0:T(8,128)}), f32[64,672]{1,0:T(8,128)}) %reduce-scatter.7.cloned.1.call-update) | async-done | bytes 172048 | tf_op jit(solution)/shard_map/reduce_scatter | solution.py:54
  608.4 1.6 convert_element_type.32
  (37 shorter events, 3.8 us)
Async XLA Ops:
  7.2 99.5 %copy-start = (bf16[672,1344]{1,0:T(8,128)(2,1)S(1)}, bf16[672,1344]{1,0:T(8,128)(2,1)}, u32[]{:S(2)}) copy-start(bf16[672,1344]{1,0:T(8,128)(2,1)} %param.9) | copy-start | bytes 5419012
  7.2 51.9 %all-gather.10.cloned.1.call-start = ((), (), s32[]{:S(2)}) async-start(), calls=%async_computation.8 | async-start | bytes 1671168 | tf_op jit(solution)/shard_map/all_gather | solution.py:70
  7.9 98.7 %all-gather.6.cloned.1.call-start = ((), (), s32[]{:S(2)}) async-start(), calls=%async_computation.4 | async-start | bytes 1671168 | tf_op jit(solution)/shard_map/all_gather | solution.py:69
  8.7 164.9 %reduce-scatter.9.cloned.1.call-start = ((), (), s32[]{:S(2)}) async-start(), calls=%async_computation.9 | async-start | bytes 6193152 | tf_op jit(solution)/shard_map/reduce_scatter | solution.py:100
  65.9 226.3 %reduce-scatter.5.cloned.1.call-start = ((), (), s32[]{:S(2)}) async-start(), calls=%async_computation.5 | async-start | bytes 12386304 | tf_op jit(solution)/shard_map/reduce_scatter | solution.py:87
  106.6 6.3 %copy-start.4 = (bf16[672,1344]{1,0:T(8,128)(2,1)S(1)}, bf16[672,1344]{1,0:T(8,128)(2,1)}, u32[]{:S(2)}) copy-start(bf16[672,1344]{1,0:T(8,128)(2,1)} %param.10) | copy-start | bytes 5419012
  106.6 6.3 %copy-start.6 = (bf16[1024,672]{1,0:T(8,128)(2,1)S(1)}, bf16[1024,672]{1,0:T(8,128)(2,1)}, u32[]{:S(2)}) copy-start(bf16[1024,672]{1,0:T(8,128)(2,1)} %all-gather.6.cloned.1.call-done) | copy-start | bytes 4128772
  128.6 0.7 copy-start.7
  128.6 1.3 copy-start.1
  128.6 215.0 %all-gather.12.cloned.1.call-start = ((), (), s32[]{:S(2)}) async-start(), calls=%async_computation.10 | async-start | bytes 3096576 | tf_op jit(solution)/shard_map/all_gather | solution.py:108
  295.2 101.4 %all-gather.14.cloned.1.call-start = ((), (), s32[]{:S(2)}) async-start(), calls=%async_computation.11 | async-start | bytes 3096576 | tf_op jit(solution)/shard_map/all_gather | solution.py:109
  295.7 153.9 %all-gather.8.cloned.1.call-start = ((), (), s32[]{:S(2)}) async-start(), calls=%async_computation.6 | async-start | bytes 3096576 | tf_op jit(solution)/shard_map/all_gather | solution.py:94
  296.5 233.7 %reduce-scatter.11.cloned.1.call-start = ((), (), s32[]{:S(2)}) async-start(), calls=%async_computation.12 | async-start | bytes 3342336 | tf_op jit(solution)/shard_map/reduce_scatter | solution.py:54
  404.2 204.2 %reduce-scatter.7.cloned.1.call-start = ((), (), s32[]{:S(2)}) async-start(), calls=%async_computation.7 | async-start | bytes 3342336 | tf_op jit(solution)/shard_map/reduce_scatter | solution.py:54
  456.3 5.6 copy-start.2
  461.9 3.7 copy-start.3
  461.9 3.7 copy-start.5
Sparse Core Ops, SparseCore 0:
  10.5 48.5 all-gather.9
  61.6 44.9 all-gather.5
  109.0 64.4 reduce-scatter.8
  175.8 116.2 reduce-scatter.4
  295.3 48.3 all-gather.11
  345.6 50.8 all-gather.13
  398.7 50.8 all-gather.7
  453.6 76.5 reduce-scatter.10
  534.3 74.1 reduce-scatter.6
where the time goes:
time: 617 us
  waiting for transfers between devices  531 us (86%)
  matrix products  51.2 us (8%)
  other arithmetic  18.1 us (3%)
  between operations  13.9 us (2%)
    reduce_scatter x2, waiting for transfers between devices, finish(): lax.psum_scatter(term(jnp.int32(0), tokens // lax.axis_size('tensor') * l...  138 us
    reduce_scatter x1, waiting for transfers between devices, local(): lax.psum_scatter(gate_term(jnp.int32(0), tok_dev * lax.axis_size('dp')),...  119 us
    dot_general x9, matrix products, contract(): lax.dot_general(left, right, (((left_dim,), (right_dim,)), ((), ())), pre...  51.2 us
    all_gather x1, waiting for transfers between devices, local(): lax.all_gather(out_grad, 'tensor', axis=0, tiled=True)  50.4 us
    all_gather x1, waiting for transfers between devices, local(): lax.all_gather(gate_delta, 'dp', axis=0, tiled=True)  46.9 us
    all_gather x1, waiting for transfers between devices, local(): lax.all_gather(up_delta, 'dp', axis=0, tiled=True)  46.8 us
    all_gather x1, waiting for transfers between devices, local(): hidden_all = lax.all_gather(hidden, 'dp', axis=0, tiled=True)  45.3 us
    reduce_scatter x1, waiting for transfers between devices, local(): lax.psum_scatter(back_term(jnp.int32(0), tok_dev * lax.axis_size('dp')),...  42.4 us
  transfers between devices with their start and end apart: 9, of which 9 were waited for; matrix products, arithmetic and copies ran while one was open for 11% of the time, Pallas kernels for 0%

commit v1 on v0

v1 whole, which is shorter than its diff:
```python
import functools

import jax
import jax.numpy as jnp
from jax import lax
from jax.experimental import pallas as pl
from jax.experimental.pallas import tpu as pltpu
from jax.sharding import PartitionSpec as P

LEN = 64
BF = jnp.bfloat16
F32 = jnp.float32
MESH = pl.DeviceIdType.MESH


def contract(left, right, left_dim, right_dim):
    return lax.dot_general(
        left, right, (((left_dim,), (right_dim,)), ((), ())), preferred_element_type=F32
    )


def kernel(
    x_ref, g_ref, wg_ref, wu_ref, wd_ref, mask_ref,
    out_ref, dx_ref, xg_out, hid_out,
    xg, hid, acc, st_a, st_b, xa, zb, acc_b, acc_a, st_z, za, st_x, xb,
    o_own, sib_st, sib_rx, st_o, o_rx,
    t_ss, t_rs, xa_ss, xa_rs, zb_ss, zb_rs, za_ss, za_rs, xb_ss, xb_rs,
    g_ss, g_rs, s_ss, s_rs, o_ss, o_rs, loc,
):
    dp = lax.axis_index("dp")
    t = lax.axis_index("tensor")
    xl, z = dp // 4, dp % 4
    xh, y, c = t // 8, (t // 2) % 4, t % 2

    def on_dp(xl_, z_):
        return (xl_ * 4 + z_, t)

    def on_tensor(xh_, y_, c_):
        return (dp, (xh_ * 4 + y_) * 2 + c_)

    x_peer = on_dp(1 - xl, z)
    z_peer = [on_dp(xl, (z + r) % 4) for r in range(4)]
    sibling = on_tensor(xh, y, 1 - c)
    chips = [((xh + i // 4) % 2, (y + i % 4) % 4) for i in range(8)]
    from_chips = [((xh + i // 4) % 2, (y + 4 - i % 4) % 4) for i in range(8)]

    def rows(slot, count=1):
        return pl.ds(pl.multiple_of(slot * LEN, LEN), count * LEN)

    def remote(src, dst, ss, rs, dev):
        return pltpu.make_async_remote_copy(
            src_ref=src, dst_ref=dst, send_sem=ss, recv_sem=rs, device_id=dev, device_id_type=MESH
        )

    bar = pltpu.get_barrier_semaphore()
    peers = [x_peer] + z_peer[1:] + [sibling] + [on_tensor(a, b, c) for a, b in chips[1:]]
    for dev in peers:
        pl.semaphore_signal(bar, inc=1, device_id=dev, device_id_type=MESH)

    my_slot = (c * 2 + xh) * 4 + y
    xg[0, rows(my_slot), :] = x_ref[...]
    xg[1, rows(my_slot), :] = g_ref[...]
    pl.semaphore_wait(bar, len(peers))

    pending = []
    mine = xg.at[:, rows(my_slot), :]
    own = []
    for i in range(1, 8):
        a, b = chips[i]
        copy = remote(mine, mine, t_ss.at[i], t_rs.at[i], on_tensor(a, b, c))
        copy.start()
        own.append(copy)
    copy = remote(mine, mine, t_ss.at[0], t_rs.at[0], sibling)
    copy.start()
    own.append(copy)
    shared = []
    for i in range(1, 8):
        own[i - 1].wait_recv()
        a, b = from_chips[i]
        part = xg.at[:, rows((c * 2 + a) * 4 + b), :]
        copy = remote(part, part, t_ss.at[7 + i], t_rs.at[7 + i], sibling)
        copy.start()
        shared.append(copy)
    own[7].wait_recv()
    for copy in shared:
        copy.wait_recv()
    pending += own + shared
    xg_copy = pltpu.make_async_copy(xg, xg_out, loc.at[0])
    xg_copy.start()

    def products(q):
        r4 = pl.ds(pl.multiple_of(q * 256, 256), 256)
        xs = xg[0, r4, :]
        acc[0] = jnp.dot(xs, wg_ref[...], preferred_element_type=F32)
        acc[1] = jnp.dot(xs, wu_ref[...], preferred_element_type=F32)
        acc[2] = contract(xg[1, r4, :], wd_ref[...], 1, 1)

    products(1 - xl)
    for k in range(3):
        st_a[k] = acc[k].astype(BF)
    to_x = []
    for r in (2, 1, 3, 0):
        part = rows((z + r) % 4)
        copy = remote(st_a.at[:, part, :], xa.at[:, part, :], xa_ss.at[r], xa_rs.at[r], x_peer)
        copy.start()
        to_x.append((r, copy))
    to_z = [[None] * 3, [None] * 3]
    for j in range(2):
        side = xl if j else 1 - xl
        products(2 + side)
        for k in range(3):
            st_b[j, k] = acc[k].astype(BF)
            acc_b[j, k] = acc[k, rows(z), :]
        for r in (2, 1, 3):
            copy = remote(
                st_b.at[j, :, rows((z + r) % 4), :], zb.at[j, r - 1],
                zb_ss.at[j * 3 + r - 1], zb_rs.at[j * 3 + r - 1], z_peer[r],
            )
            copy.start()
            to_z[j][r - 1] = copy
    products(xl)
    pairs = []
    for r, copy in to_x:
        copy.wait_recv()
        part = rows((z + r) % 4)
        if r:
            for k in range(3):
                st_z[r - 1, k] = (acc[k, part, :] + xa[k, part, :].astype(F32)).astype(BF)
            pair = remote(st_z.at[r - 1], za.at[r - 1], za_ss.at[r - 1], za_rs.at[r - 1], z_peer[r])
            pair.start()
            pairs.append(pair)
        else:
            for k in range(3):
                acc_a[k] = acc[k, part, :] + xa[k, part, :].astype(F32)
    pending_send = [copy for _, copy in to_x] + to_z[0] + to_z[1] + pairs

    for copy in to_z[0]:
        copy.wait_recv()
    for k in range(3):
        st_x[k] = acc_b[0, k] + (
            zb[0, 0, k].astype(F32) + zb[0, 1, k].astype(F32) + zb[0, 2, k].astype(F32)
        )
    to_xb = remote(st_x, xb, xb_ss.at[0], xb_rs.at[0], x_peer)
    to_xb.start()
    pending_send.append(to_xb)

    def activate(base, parts, extra, which, slot):
        def step(i, carry):
            rr = pl.ds(pl.multiple_of(i * 16, 16), 16)

            def total(k):
                v = base(k, rr)
                for p in range(3):
                    v = v + parts(p, k, rr).astype(F32)
                return v if extra is None else v + extra[k, rr, :]

            gate_pre, up_pre, hidden_grad = total(0), total(1), total(2)
            keep = mask_ref[which]
            sig = jax.nn.sigmoid(gate_pre)
            act = gate_pre * sig
            dst = pl.ds(pl.multiple_of(slot * LEN + i * 16, 16), 16)
            hid[0, dst, :] = (act * up_pre * keep).astype(BF)
            hid[1, dst, :] = (
                hidden_grad * up_pre * sig * (1.0 + gate_pre * (1.0 - sig)) * keep
            ).astype(BF)
            hid[2, dst, :] = (hidden_grad * act * keep).astype(BF)
            return carry

        lax.fori_loop(0, LEN // 16, step, 0)

    def give(slot, sem, dev):
        part = hid.at[:, rows(slot), :]
        copy = remote(part, part, g_ss.at[sem], g_rs.at[sem], dev)
        copy.start()
        pending_send.append(copy)
        return copy

    slot_a, slot_b = 4 * xl + z, 8 + 4 * xl + z
    for copy in pairs:
        copy.wait_recv()
    activate(
        lambda k, rr: acc_a[k, rr, :], lambda p, k, rr: za[p, k, rr, :], None, 0, slot_a
    )
    a_z = {r: give(slot_a, r - 1, z_peer[r]) for r in (2, 1, 3)}
    a_x = {0: give(slot_a, 3, x_peer)}
    for copy in to_z[1]:
        copy.wait_recv()
    to_xb.wait_recv()
    activate(
        lambda k, rr: acc_b[1, k, rr, :], lambda p, k, rr: zb[1, p, k, rr, :], xb, 1, slot_b
    )
    b_x = give(slot_b, 7, x_peer)
    b_z = {r: give(slot_b, 7 + r, z_peer[r]) for r in (2, 1, 3)}
    for r in (1, 3, 2):
        a_z[r].wait_recv()
        a_x[r] = give(4 * xl + (z + 4 - r) % 4, 3 + r, x_peer)
    b_x.wait_recv()
    b_f = {r: give(8 + 4 * (1 - xl) + z, 10 + r, z_peer[r]) for r in (2, 1, 3)}

    hid_copies = []
    o_sends = []

    def outputs(n, core, q, side):
        r4 = pl.ds(pl.multiple_of(q * 256, 256), 256)
        keep = pltpu.make_async_copy(hid.at[:, r4, :], hid_out.at[:, r4, :], loc.at[1 + n])
        keep.start()
        hid_copies.append(keep)
        o = jnp.dot(hid[0, r4, :], wd_ref[...], preferred_element_type=F32)
        d = contract(hid[1, r4, :], wg_ref[...], 1, 1) + contract(hid[2, r4, :], wu_ref[...], 1, 1)
        m = n // 2
        to_sib = remote(sib_st.at[m], sib_rx.at[m], s_ss.at[m], s_rs.at[m], sibling)

        mine_at = jnp.where(c == core, 2, m)
        sib_st[mine_at, 0] = o
        sib_st[mine_at, 1] = d

        @pl.when(c != core)
        def _():
            to_sib.start()

        far = (side + xh) % 2

        @pl.when(c == core)
        def _():
            to_sib.wait_recv()
            for k in range(2):
                st_o[m, k] = (sib_st[2, k] + sib_rx[m, k]).astype(BF)

            @pl.when(far == 0)
            def _():
                for k in range(2):
                    o_own[k] = sib_st[2, k, rows(y), :] + sib_rx[m, k, rows(y), :]

        for r in (2, 1, 3, 0):
            yy = (y + r) % 4
            send = remote(
                st_o.at[m, :, rows(yy), :], o_rx.at[far * 4 + r],
                o_ss.at[m * 4 + r], o_rs.at[far * 4 + r], on_tensor(side, yy, c),
            )
            ok = (c == core) if r else ((c == core) & (far == 1))

            @pl.when(ok)
            def _(send=send):
                send.start()

            o_sends.append((ok, send))
        return (c != core), to_sib

    sib = []
    sib.append(outputs(0, 0, xl, xl))
    for r in (1, 2, 3):
        b_z[r].wait_recv()
    sib.append(outputs(1, 1, 2 + xl, xl))
    for r in (1, 2, 3):
        b_f[r].wait_recv()
    sib.append(outputs(2, 1, 3 - xl, 1 - xl))
    for r in range(4):
        a_x[r].wait_recv()
    sib.append(outputs(3, 0, 1 - xl, 1 - xl))

    for i in range(1, 8):
        remote(st_o.at[0, :, rows(0), :], o_rx.at[i], o_ss.at[0], o_rs.at[i], sibling).wait_recv()
    for k, ref in ((0, out_ref), (1, dx_ref)):
        v = o_own[k]
        for i in range(1, 8):
            v = v + o_rx[i, k].astype(F32)
        ref[...] = v.astype(BF)

    for copy in pending + pending_send:
        copy.wait_send()
    for ok, send in o_sends + sib:
        @pl.when(ok)
        def _(send=send):
            send.wait_send()
    xg_copy.wait()
    for copy in hid_copies:
        copy.wait()


def local(layer_input, gate_weight, up_weight, down_weight, granularity, out_grad):
    feat, cols = gate_weight.shape
    t = lax.axis_index("tensor")
    dp = lax.axis_index("dp")
    tokens = 16 * LEN
    slots = jnp.stack([dp, 8 + dp])
    seqs = ((slots // 4) % 2 * 4 + slots % 4) * 2 + slots // 8
    widths = jnp.left_shift(jnp.int32(2688), jnp.take(granularity, seqs))
    col = t * cols + jnp.arange(cols, dtype=jnp.int32)
    mask = (col[None, None, :] < widths[:, None, None]).astype(F32)

    vm = pl.BlockSpec(memory_space=pltpu.VMEM)
    hbm = pl.BlockSpec(memory_space=pl.ANY)
    seq3 = (3, LEN, cols)
    dma = pltpu.SemaphoreType.DMA
    out, dx, xg, hid = pl.pallas_call(
        kernel,
        out_shape=(
            jax.ShapeDtypeStruct((LEN, feat), BF),
            jax.ShapeDtypeStruct((LEN, feat), BF),
            jax.ShapeDtypeStruct((2, tokens, feat), BF),
            jax.ShapeDtypeStruct((3, tokens, cols), BF),
        ),
        in_specs=[vm] * 6,
        out_specs=(vm, vm, hbm, hbm),
        scratch_shapes=[
            pltpu.VMEM((2, tokens, feat), BF),
            pltpu.VMEM((3, tokens, cols), BF),
            pltpu.VMEM((3, 256, cols), F32),
            pltpu.VMEM((3, 256, cols), BF),
            pltpu.VMEM((2, 3, 256, cols), BF),
            pltpu.VMEM((3, 256, cols), BF),
            pltpu.VMEM((2, 3) + seq3, BF),
            pltpu.VMEM((2,) + seq3, F32),
            pltpu.VMEM(seq3, F32),
            pltpu.VMEM((3,) + seq3, BF),
            pltpu.VMEM((3,) + seq3, BF),
            pltpu.VMEM(seq3, F32),
            pltpu.VMEM(seq3, F32),
            pltpu.VMEM((2, LEN, feat), F32),
            pltpu.VMEM((3, 2, 256, feat), F32),
            pltpu.VMEM((2, 2, 256, feat), F32),
            pltpu.VMEM((2, 2, 256, feat), BF),
            pltpu.VMEM((8, 2, LEN, feat), BF),
            dma((15,)), dma((15,)),
            dma((4,)), dma((4,)),
            dma((6,)), dma((6,)),
            dma((3,)), dma((3,)),
            dma((1,)), dma((1,)),
            dma((14,)), dma((14,)),
            dma((2,)), dma((2,)),
            dma((8,)), dma((8,)),
            dma((5,)),
        ],
        compiler_params=pltpu.CompilerParams(
            collective_id=0, has_side_effects=True, vmem_limit_bytes=62 << 20
        ),
        cost_estimate=pl.CostEstimate(flops=12_000_000_000, bytes_accessed=20_000_000, transcendentals=0),
    )(layer_input, out_grad, gate_weight, up_weight, down_weight, mask)
    down_grad = contract(hid[0], xg[1], 0, 0).astype(BF)
    gate_grad = contract(xg[0], hid[1], 0, 0).astype(BF)
    up_grad = contract(xg[0], hid[2], 0, 0).astype(BF)
    return out, dx, gate_grad, up_grad, down_grad


def solution(mesh):
    in_specs = (
        P("tensor", "dp"),
        P("dp", "tensor"),
        P("dp", "tensor"),
        P("tensor", "dp"),
        P(),
        P("tensor", "dp"),
    )
    out_specs = (
        P("tensor", "dp"),
        P("tensor", "dp"),
        P("dp", "tensor"),
        P("dp", "tensor"),
        P("tensor", "dp"),
    )
    return jax.shard_map(local, mesh=mesh, in_specs=in_specs, out_specs=out_specs, check_vma=False)
```

time: 617 us -> 228 us (0.37)
  waiting for transfers between devices: 531 us -> 0 us
  Pallas kernels: 0 us -> 204 us
  matrix products: 51.2 us -> 13.3 us
  other arithmetic: 18.1 us -> 0.89 us
  between operations: 13.9 us -> 0.69 us
    reduce_scatter x4 -> x0, waiting for transfers between devices: 299 us -> none  [the longest x2 138 us: finish(): lax.psum_scatter(term(jnp.int32(0), tokens // lax.axis_size('tensor') * l...]
    all_gather x5 -> x0, waiting for transfers between devices: 230 us -> none  [the longest x1 50.4 us: local(): lax.all_gather(out_grad, 'tensor', axis=0, tiled=True)]
    pallas_call x0 -> x1, Pallas kernels: none -> 204 us  [local(): pl.pallas_call(kernel, out_shape=(jax.ShapeDtypeStruct((LEN, feat), BF),...]
    dot_general x9 -> x3, matrix products: 51.2 us -> 13.3 us  [contract(): lax.dot_general(left, right, (((left_dim,), (right_dim,)), ((), ())), pre...]
    concatenate x1 -> x0, other arithmetic: 10.7 us -> none  [gate_product(): jnp.concatenate([contract(segment[0], gate_weight, 1, 0), contract(segmen...]
  transfers between devices with their start and end apart: 9 -> 0, of which waited for: 9 -> 0; matrix products, arithmetic and copies ran while one was open for 11% -> 0% of each run, Pallas kernels for 0% -> 0%
where the time goes in v1:
time: 228 us; the launch traced here: 225 us
  Pallas kernels  204 us (89%)
  matrix products  13.3 us (6%)
  local copies, waits for them, and re-layouts  6.33 us (3%)
    pallas_call x1, Pallas kernels, local(): pl.pallas_call(kernel, out_shape=(jax.ShapeDtypeStruct((LEN, feat), BF),...  204 us
    dot_general x3, matrix products, contract(): lax.dot_general(left, right, (((left_dim,), (right_dim,)), ((), ())), pre...  13.3 us
    unnamed x13, local copies, waits for them, and re-layouts  5.7 us

profile of v1, /device:TPU:0, one launch (start us, length us, event | category | flops | bytes accessed | tf_op | source)
XLA Modules:
  0.0 225.4 jit_solution(10092770898737440805)
XLA Ops:
  0.6 0.0 copy-start
  0.7 0.1 fusion.18
  0.8 0.5 copy-done
  1.3 0.6 gather_fusion
  1.9 0.1 fusion.19
  2.0 0.7 compare_convert_fusion.mask_ref
  2.7 3.9 %copy.12.wd_ref = bf16[1344,672]{1,0:T(8,128)(2,1)} copy(bf16[1344,672]{0,1:T(8,128)(2,1)} %param.9) | data formatting | bytes 3612672 | tf_op args[3]
  6.6 204.2 %shard_map.101 = (bf16[64,672]{1,0:T(8,128)(2,1)}, bf16[64,672]{1,0:T(8,128)(2,1)}, bf16[2,1024,672]{2,1,0:T(8,128)(2,1)}, bf16[3,1024,1344]{2,1,0:T(8,128)(2,1)}) custom-call(bf16[64,672]{1,0:T(8,128)(2,1)} %x_ref.1, bf16[64,672]{1,0:T(8,128)(2,1)} %g_ref.1, bf16[672,1344]{1,0:T(8,128)(2,1)} %wg_ref.1, bf16[672,1344]{1,0:T(8,128)(2,1)} %wu_ref.1, ...), custom_call_target="tpu_custom_call" | custom-call | flops 12000000000 | bytes 20000000 | tf_op jit(solution)/shard_map/pallas_call | solution.py:295
  210.8 0.0 copy-start.3
  210.8 0.0 copy-start.4
  210.9 6.0 %convolution_convert_fusion.1 = bf16[672,1344]{1,0:T(8,128)(2,1)} fusion(bf16[3,1024,1344]{2,1,0:T(8,128)(2,1)} %get-tuple-element.12, bf16[2,1024,672]{2,1,0:T(8,128)(2,1)} %get-tuple-element.11), kind=kOutput, calls=%fused_computation.2 | convolution fusion | flops 1850591232 | bytes 6262784 | tf_op jit(solution)/shard_map/dot_general | solution.py:17
  216.9 0.0 copy-done.3
  216.9 0.0 copy-done.4
  216.9 3.7 %convolution_convert_fusion = bf16[1344,672]{0,1:T(8,128)(2,1)} fusion(bf16[3,1024,1344]{2,1,0:T(8,128)(2,1)S(1)} %copy-done.3, bf16[2,1024,672]{2,1,0:T(8,128)(2,1)S(1)} %copy-done.4), kind=kOutput, calls=%fused_computation.1 | convolution fusion | flops 1850591232 | bytes 6262784 | tf_op jit(solution)/shard_map/dot_general | solution.py:17
  220.5 0.0 copy-start.2
  220.5 0.0 copy-start.1
  220.5 3.6 %convolution_convert_fusion.2 = bf16[672,1344]{1,0:T(8,128)(2,1)} fusion(bf16[3,1024,1344]{2,1,0:T(8,128)(2,1)S(1)} %copy-done.3, bf16[2,1024,672]{2,1,0:T(8,128)(2,1)S(1)} %copy-done.4), kind=kOutput, calls=%fused_computation.3 | convolution fusion | flops 1850591232 | bytes 6262784 | tf_op jit(solution)/shard_map/dot_general | solution.py:17
  224.2 0.0 copy-done.2
  224.2 0.6 copy.15
  224.8 0.0 copy-done.1
  224.8 0.6 copy.16
  (2 shorter events, 0.0 us)
Async XLA Ops:
  0.6 0.7 copy-start
  210.8 6.0 %copy-start.3 = (bf16[3,1024,1344]{2,1,0:T(8,128)(2,1)S(1)}, bf16[3,1024,1344]{2,1,0:T(8,128)(2,1)}, u32[]{:S(2)}) copy-start(bf16[3,1024,1344]{2,1,0:T(8,128)(2,1)} %get-tuple-element.12) | copy-start | bytes 24772612
  210.8 6.0 %copy-start.4 = (bf16[2,1024,672]{2,1,0:T(8,128)(2,1)S(1)}, bf16[2,1024,672]{2,1,0:T(8,128)(2,1)}, u32[]{:S(2)}) copy-start(bf16[2,1024,672]{2,1,0:T(8,128)(2,1)} %get-tuple-element.11) | copy-start | bytes 8257540
  220.5 3.6 %copy-start.2 = (bf16[64,672]{1,0:T(8,128)(2,1)S(1)}, bf16[64,672]{1,0:T(8,128)(2,1)}, u32[]{:S(2)}) copy-start(bf16[64,672]{1,0:T(8,128)(2,1)} %get-tuple-element.18) | copy-start | bytes 258052
  220.5 4.3 %copy-start.1 = (bf16[64,672]{1,0:T(8,128)(2,1)S(1)}, bf16[64,672]{1,0:T(8,128)(2,1)}, u32[]{:S(2)}) copy-start(bf16[64,672]{1,0:T(8,128)(2,1)} %get-tuple-element.19) | copy-start | bytes 258052

commit v2 on v0

v2 whole, which is shorter than its diff:
```python
import jax
import jax.numpy as jnp
from jax import lax
from jax.experimental import pallas as pl
from jax.experimental.pallas import tpu as pltpu
from jax.sharding import PartitionSpec as P

LEN = 64
BF = jnp.bfloat16
F32 = jnp.float32
MESH = pl.DeviceIdType.MESH


def contract(left, right, left_dim, right_dim):
    return lax.dot_general(
        left, right, (((left_dim,), (right_dim,)), ((), ())), preferred_element_type=F32
    )


def kernel(
    gran_ref, x_ref, g_ref, wg_ref, wu_ref, wd_ref,
    out_ref, dx_ref, xg_out, hid_out,
    xg, hid, acc, keep, st_a, xa, st_b, zb, st_c, zc, st_z, za, st_x, xb,
    o_own, sib_st, sib_rx, st_y, y_rx, st_w, w_rx, ss, rs, loc,
):
    cols = wg_ref.shape[1]
    dp = lax.axis_index("dp")
    t = lax.axis_index("tensor")
    xl, z = dp // 4, dp % 4
    xh, y, c = t // 8, (t // 2) % 4, t % 2
    zp, zf, zm = (z + 1) % 4, (z + 2) % 4, (z + 3) % 4

    def on_tensor(xh_, y_, c_):
        return (dp, (xh_ * 4 + y_ % 4) * 2 + c_)

    x_peer = ((1 - xl) * 4 + z, t)
    z_peer = [(xl * 4 + (z + r) % 4, t) for r in range(4)]
    sibling = on_tensor(xh, y, 1 - c)
    far_chip = on_tensor(1 - xh, y, c)
    y_chip = [on_tensor(xh, y + r, c) for r in range(4)]
    y_of = (0, 3, 1, 2)

    sends = []

    def send(src, dst, dev):
        i = len(sends)
        copy = pltpu.make_async_remote_copy(
            src_ref=src, dst_ref=dst, send_sem=ss.at[i], recv_sem=rs.at[i],
            device_id=dev, device_id_type=MESH,
        )
        copy.start()
        sends.append(copy)
        return copy

    def got(*copies):
        for copy in copies:
            copy.wait_recv()

    def r16(i, base=0):
        return pl.ds(pl.multiple_of(base + i * 16, 16), 16)

    def r64(i, base=0):
        return pl.ds(pl.multiple_of(base + i * LEN, LEN), LEN)

    bar = pltpu.get_barrier_semaphore()
    peers = [x_peer, sibling, far_chip] + z_peer[1:] + y_chip[1:]
    for dev in peers:
        pl.semaphore_signal(bar, inc=1, device_id=dev, device_id_type=MESH)
    xg[0, 0:LEN, :] = x_ref[...]
    xg[1, 0:LEN, :] = g_ref[...]
    pl.semaphore_wait(bar, len(peers))

    def seqs(p, k, n=1):
        return xg.at[:, pl.ds(p * 256 + k * LEN, n * LEN), :]

    mine, theirs = seqs(0, 0), seqs(0, 1)
    i_far = send(mine, seqs(0, 1), far_chip)
    i_sib = send(mine, seqs(0, 2), sibling)
    i_y = {1: send(mine, seqs(1, 0), y_chip[1]), 2: send(mine, seqs(2, 0), y_chip[3])}
    i_y[3] = send(mine, seqs(3, 0), y_chip[2])
    got(i_far)
    i_sib2 = send(theirs, seqs(0, 3), sibling)
    i_y2 = {1: send(theirs, seqs(1, 1), y_chip[1]), 2: send(theirs, seqs(2, 1), y_chip[3])}
    i_y2[3] = send(theirs, seqs(3, 1), y_chip[2])
    i_s = {}
    local_copies = []

    def keep_in_hbm(src, dst):
        copy = pltpu.make_async_copy(src, dst, loc.at[len(local_copies)])
        copy.start()
        local_copies.append(copy)

    def gather(p):
        if p == 0:
            got(i_sib, i_sib2)
        else:
            got(i_y[p], i_y2[p])
            i_s[p] = send(seqs(p, 0, 2), seqs(p, 2, 2), sibling)
            got(i_s[p])
        keep_in_hbm(seqs(p, 0, 4), xg_out.at[:, pl.ds(p * 256, 256), :])

    s_a, s_b, s_c, s_z, s_x = {}, {}, {}, {}, {}

    def products(p):
        gather(p)
        xs = xg[0, p * 256 : p * 256 + 256, :]
        gs = xg[1, p * 256 : p * 256 + 256, :]
        acc[0] = jnp.dot(xs, wg_ref[...], preferred_element_type=F32)
        acc[1] = jnp.dot(xs, wu_ref[...], preferred_element_type=F32)
        acc[2] = jnp.dot(gs, wd_ref[...], preferred_element_type=F32)
        for k in range(3):
            st_a[p, k] = acc[k, r64(1 - xl), :].astype(BF)
        s_a[p] = send(st_a.at[p], xa.at[p], x_peer)
        for k in range(3):
            st_b[p, 0, k, 0:16, :] = acc[k, r16(zf, 128), :].astype(BF)
            st_b[p, 0, k, 16:32, :] = acc[k, r16(zp, 192), :].astype(BF)
            st_b[p, 1, k, 0:16, :] = acc[k, r16(zf, 192), :].astype(BF)
            st_b[p, 1, k, 16:32, :] = acc[k, r16(zm, 128), :].astype(BF)
        s_b[p] = (
            send(st_b.at[p, 0], zb.at[p, 0], z_peer[1]),
            send(st_b.at[p, 1], zb.at[p, 1], z_peer[3]),
        )
        for k in range(3):
            keep[p, k, 0:64, :] = acc[k, r64(xl), :]
            keep[p, k, 64:80, :] = acc[k, r16(zp, 128), :]
            keep[p, k, 80:96, :] = acc[k, r16(zm, 192), :]
            keep[p, k, 96:112, :] = acc[k, r16(z, 128), :]
            keep[p, k, 112:128, :] = acc[k, r16(z, 192), :]

    def second(p):
        sent = []
        for d, peer in ((0, z_peer[1]), (1, z_peer[3])):
            got(s_b[p][d])
            for k in range(3):
                st_c[p, d, k] = (
                    keep[p, k, 64 + 16 * d : 80 + 16 * d, :] + zb[p, d, k, 0:16, :].astype(F32)
                ).astype(BF)
            sent.append(send(st_c.at[p, d], zc.at[p, d], peer))
        s_c[p] = sent
        got(s_a[p])
        sent = []
        for r in (2, 1, 3):
            zz = r16((z + r) % 4)
            for k in range(3):
                st_z[p, r - 1, k] = (keep[p, k, zz, :] + xa[p, k, zz, :].astype(F32)).astype(BF)
            sent.append(send(st_z.at[p, r - 1], za.at[p, r - 1], z_peer[r]))
        s_z[p] = sent

    def third(p):
        got(*s_c[p])
        for k in range(3):
            v0 = keep[p, k, 96:112, :] + zc[p, 0, k].astype(F32) + zb[p, 1, k, 16:32, :].astype(F32)
            v1 = keep[p, k, 112:128, :] + zc[p, 1, k].astype(F32) + zb[p, 0, k, 16:32, :].astype(F32)
            st_x[p, k] = jnp.where(xl == 0, v1, v0).astype(BF)
            keep[p, k, 64:80, :] = jnp.where(xl == 0, v0, v1)
        s_x[p] = send(st_x.at[p], xb.at[p], x_peer)

    def activate(p, k, total):
        seq = ((xh + xl) % 2 * 4 + (y + y_of[p]) % 4) * 2 + (c + k // 2) % 2
        level = gran_ref[seq]
        width = jnp.where(
            level == 0, 2688, jnp.where(level == 1, 5376, jnp.where(level == 2, 10752, 21504))
        )
        col = t * cols + lax.broadcasted_iota(jnp.int32, (1, cols), 1)
        mask = jnp.where(col < width, 1.0, 0.0).astype(F32)
        gate_pre, up_pre, hidden_grad = total(0), total(1), total(2)
        sig = jax.nn.sigmoid(gate_pre)
        act = gate_pre * sig
        at = 4 * p + k + xl
        hid[0, at, r16(z), :] = (act * up_pre * mask).astype(BF)
        hid[1, at, r16(z), :] = (
            hidden_grad * up_pre * sig * (1.0 + gate_pre * (1.0 - sig)) * mask
        ).astype(BF)
        hid[2, at, r16(z), :] = (hidden_grad * act * mask).astype(BF)

    h_az, h_ax, h_bx, h_bz, h_bf = {}, {}, {}, {}, {}

    def share(src, dev):
        return send(src, src, dev)

    def owned(p):
        got(*s_z[p])

        def total_a(k):
            v = keep[p, k, r16(z), :] + xa[p, k, r16(z), :].astype(F32)
            for r in range(3):
                v = v + za[p, r, k].astype(F32)
            return v

        activate(p, 0, total_a)
        part = hid.at[:, 4 * p + xl, r16(z), :]
        h_az[p] = [share(part, z_peer[r]) for r in (2, 1, 3)]
        got(s_x[p])
        activate(p, 2, lambda k: keep[p, k, 64:80, :] + xb[p, k].astype(F32))
        h_bx[p] = share(hid.at[:, 4 * p + 2 + xl, r16(z), :], x_peer)

    def spread(p):
        got(h_bx[p])
        part = hid.at[:, pl.ds(4 * p + 2, 2), r16(z), :]
        h_bz[p] = (share(part, z_peer[1]), share(part, z_peer[3]))
        got(*h_az[p])
        h_ax[p] = share(hid.at[:, 4 * p + xl], x_peer)

    def forward(p):
        got(h_bz[p][0])
        one = share(hid.at[:, 4 * p + 2, r16(zm), :], z_peer[1])
        got(h_bz[p][1])
        two = share(hid.at[:, 4 * p + 3, r16(zp), :], z_peer[3])
        h_bf[p] = (one, two)

    s_o, s_y = {}, {}

    def outputs(p):
        got(h_ax[p], *h_bf[p])
        keep_in_hbm(hid.at[:, pl.ds(4 * p, 4)], hid_out.at[:, pl.ds(4 * p, 4)])
        h, gd, ud = (hid[i, 4 * p : 4 * p + 4].reshape(256, cols) for i in range(3))
        o = contract(h, wd_ref[...], 1, 1)
        d = contract(gd, wg_ref[...], 1, 1) + contract(ud, wu_ref[...], 1, 1)
        for i, v in ((0, o), (1, d)):
            sib_st[p, i] = v[128:, :]
            o_own[p % 2, i] = v[:128, :]
        s_o[p] = send(sib_st.at[p], sib_rx.at[p], sibling)

    def between_cores(p):
        got(s_o[p])
        if p == 0:
            o_own[0] = o_own[0] + sib_rx[0]
        else:
            st_y[p - 1] = (o_own[p % 2] + sib_rx[p]).astype(BF)
            s_y[p] = send(st_y.at[p - 1], y_rx.at[p - 1], y_chip[y_of[p]])

    products(0)
    products(1)
    second(0)
    products(2)
    second(1)
    third(0)
    third(1)
    owned(1)
    second(2)
    spread(1)
    products(3)
    third(2)
    forward(1)
    owned(2)
    second(3)
    spread(2)
    outputs(1)
    third(3)
    forward(2)
    between_cores(1)
    owned(3)
    owned(0)
    outputs(2)
    spread(3)
    spread(0)
    between_cores(2)
    forward(3)
    forward(0)
    outputs(3)
    between_cores(3)
    outputs(0)
    between_cores(0)

    got(s_y[1], s_y[2], s_y[3])
    for i in range(2):
        v = o_own[0, i]
        for p in range(3):
            v = v + y_rx[p, i].astype(F32)
        o_own[0, i] = v
        st_w[i] = v[LEN:, :].astype(BF)
    got(send(st_w, w_rx, far_chip))
    out_ref[...] = (o_own[0, 0, 0:LEN, :] + w_rx[0].astype(F32)).astype(BF)
    dx_ref[...] = (o_own[0, 1, 0:LEN, :] + w_rx[1].astype(F32)).astype(BF)

    for copy in sends:
        copy.wait_send()
    for copy in local_copies:
        copy.wait()
    assert len(sends) == N_SENDS


N_SENDS = 12 + 4 * 19 + 3 + 1


def local(layer_input, gate_weight, up_weight, down_weight, granularity, out_grad):
    feat, cols = gate_weight.shape
    vm = pl.BlockSpec(memory_space=pltpu.VMEM)
    hbm = pl.BlockSpec(memory_space=pl.ANY)
    sm = pl.BlockSpec(memory_space=pltpu.SMEM)
    out, dx, xg, hid = pl.pallas_call(
        kernel,
        out_shape=(
            jax.ShapeDtypeStruct((LEN, feat), BF),
            jax.ShapeDtypeStruct((LEN, feat), BF),
            jax.ShapeDtypeStruct((2, 1024, feat), BF),
            jax.ShapeDtypeStruct((3, 16, LEN, cols), BF),
        ),
        in_specs=[sm] + [vm] * 5,
        out_specs=(vm, vm, hbm, hbm),
        scratch_shapes=[
            pltpu.VMEM((2, 1024, feat), BF),
            pltpu.VMEM((3, 16, LEN, cols), BF),
            pltpu.VMEM((3, 256, cols), F32),
            pltpu.VMEM((4, 3, 128, cols), F32),
            pltpu.VMEM((4, 3, LEN, cols), BF),
            pltpu.VMEM((4, 3, LEN, cols), BF),
            pltpu.VMEM((4, 2, 3, 32, cols), BF),
            pltpu.VMEM((4, 2, 3, 32, cols), BF),
            pltpu.VMEM((4, 2, 3, 16, cols), BF),
            pltpu.VMEM((4, 2, 3, 16, cols), BF),
            pltpu.VMEM((4, 3, 3, 16, cols), BF),
            pltpu.VMEM((4, 3, 3, 16, cols), BF),
            pltpu.VMEM((4, 3, 16, cols), BF),
            pltpu.VMEM((4, 3, 16, cols), BF),
            pltpu.VMEM((2, 2, 128, feat), F32),
            pltpu.VMEM((4, 2, 128, feat), F32),
            pltpu.VMEM((4, 2, 128, feat), F32),
            pltpu.VMEM((3, 2, 128, feat), BF),
            pltpu.VMEM((3, 2, 128, feat), BF),
            pltpu.VMEM((2, LEN, feat), BF),
            pltpu.VMEM((2, LEN, feat), BF),
            pltpu.SemaphoreType.DMA((N_SENDS,)),
            pltpu.SemaphoreType.DMA((N_SENDS,)),
            pltpu.SemaphoreType.DMA((8,)),
        ],
        compiler_params=pltpu.CompilerParams(
            collective_id=0, has_side_effects=True, vmem_limit_bytes=62 << 20
        ),
        cost_estimate=pl.CostEstimate(flops=12_000_000_000, bytes_accessed=20_000_000, transcendentals=0),
    )(granularity, layer_input, out_grad, gate_weight, up_weight, down_weight.T)
    hid = hid.reshape(3, 1024, cols)
    down_grad = contract(xg[1], hid[0], 0, 0).astype(BF).T
    gate_grad = contract(xg[0], hid[1], 0, 0).astype(BF)
    up_grad = contract(xg[0], hid[2], 0, 0).astype(BF)
    return out, dx, gate_grad, up_grad, down_grad


def solution(mesh):
    in_specs = (
        P("tensor", "dp"),
        P("dp", "tensor"),
        P("dp", "tensor"),
        P("tensor", "dp"),
        P(),
        P("tensor", "dp"),
    )
    out_specs = (
        P("tensor", "dp"),
        P("tensor", "dp"),
        P("dp", "tensor"),
        P("dp", "tensor"),
        P("tensor", "dp"),
    )
    return jax.shard_map(local, mesh=mesh, in_specs=in_specs, out_specs=out_specs, check_vma=False)
```

time: 617 us -> 184 us (0.30)
  waiting for transfers between devices: 531 us -> 0 us
  Pallas kernels: 0 us -> 165 us
  matrix products: 51.2 us -> 10.9 us
  other arithmetic: 18.1 us -> 0 us
  between operations: 13.9 us -> 0.66 us
    reduce_scatter x4 -> x0, waiting for transfers between devices: 299 us -> none  [the longest x2 138 us: finish(): lax.psum_scatter(term(jnp.int32(0), tokens // lax.axis_size('tensor') * l...]
    all_gather x5 -> x0, waiting for transfers between devices: 230 us -> none  [the longest x1 50.4 us: local(): lax.all_gather(out_grad, 'tensor', axis=0, tiled=True)]
    pallas_call x0 -> x1, Pallas kernels: none -> 165 us  [local(): pl.pallas_call(kernel, out_shape=(jax.ShapeDtypeStruct((LEN, feat), BF),...]
    dot_general x9 -> x3, matrix products: 51.2 us -> 10.9 us  [contract(): lax.dot_general(left, right, (((left_dim,), (right_dim,)), ((), ())), pre...]
    concatenate x1 -> x0, other arithmetic: 10.7 us -> none  [gate_product(): jnp.concatenate([contract(segment[0], gate_weight, 1, 0), contract(segmen...]
  transfers between devices with their start and end apart: 9 -> 0, of which waited for: 9 -> 0; matrix products, arithmetic and copies ran while one was open for 11% -> 0% of each run, Pallas kernels for 0% -> 0%
where the time goes in v2:
time: 184 us; the launch traced here: 182 us
  Pallas kernels  165 us (90%)
  matrix products  10.9 us (6%)
  local copies, waits for them, and re-layouts  5.7 us (3%)
    pallas_call x1, Pallas kernels, local(): pl.pallas_call(kernel, out_shape=(jax.ShapeDtypeStruct((LEN, feat), BF),...  165 us
    dot_general x3, matrix products, contract(): lax.dot_general(left, right, (((left_dim,), (right_dim,)), ((), ())), pre...  10.9 us
    slice x1, local copies, waits for them, and re-layouts, local(): down_grad = contract(xg[1], hid[0], 0, 0).astype(BF).T  4.24 us

profile of v2, /device:TPU:0, one launch (start us, length us, event | category | flops | bytes accessed | tf_op | source)
XLA Modules:
  0.0 182.1 jit_solution(2642780452575015328)
XLA Ops:
  0.6 164.8 %shard_map.101 = (bf16[64,672]{1,0:T(8,128)(2,1)}, bf16[64,672]{1,0:T(8,128)(2,1)}, bf16[2,1024,672]{2,1,0:T(8,128)(2,1)}, bf16[3,16,64,1344]{3,2,1,0:T(8,128)(2,1)}) custom-call(s32[16]{0:T(128)} %gran_ref.1, bf16[64,672]{1,0:T(8,128)(2,1)} %x_ref.1, bf16[64,672]{1,0:T(8,128)(2,1)} %g_ref.1, bf16[672,1344]{1,0:T(8,128)(2,1)} %wg_ref.1, ...), custom_call_target="tpu_custom_call" | custom-call | flops 12000000000 | bytes 20000000 | tf_op jit(solution)/shard_map/pallas_call | solution.py:291
  165.5 0.0 copy-start.2
  165.5 4.2 %fusion.6 = (bf16[1,16,64,1344]{3,2,1,0:T(8,128)(2,1)S(1)}, bf16[1,16,64,1344]{3,2,1,0:T(8,128)(2,1)S(1)}, bf16[1,16,64,1344]{3,2,1,0:T(8,128)(2,1)S(1)}) fusion(bf16[3,16,64,1344]{3,2,1,0:T(8,128)(2,1)} %get-tuple-element.12), kind=kLoop, calls=%fused_computation.9 | loop fusion | bytes 16515072 | tf_op jit(solution)/shard_map/slice | solution.py:333
  169.7 0.2 copy-done.2
  169.9 3.7 %convolution_convert_fusion = bf16[1344,672]{0,1:T(8,128)(2,1)} fusion(bf16[1024,1344]{1,0:T(8,128)(2,1)S(1)} %bitcast.17, bf16[2,1024,672]{2,1,0:T(8,128)(2,1)S(1)} %copy-done.2), kind=kOutput, calls=%fused_computation | convolution fusion | flops 1850591232 | bytes 6262784 | tf_op jit(solution)/shard_map/dot_general | solution.py:15
  173.6 3.6 %convolution_convert_fusion.1 = bf16[672,1344]{1,0:T(8,128)(2,1)} fusion(bf16[1024,1344]{1,0:T(8,128)(2,1)S(1)} %bitcast.16, bf16[2,1024,672]{2,1,0:T(8,128)(2,1)S(1)} %copy-done.2), kind=kOutput, calls=%fused_computation.1 | convolution fusion | flops 1850591232 | bytes 6262784 | tf_op jit(solution)/shard_map/dot_general | solution.py:15
  177.2 0.0 copy-start.1
  177.2 0.0 copy-start
  177.2 3.6 %convolution_convert_fusion.2 = bf16[672,1344]{1,0:T(8,128)(2,1)} fusion(bf16[1024,1344]{1,0:T(8,128)(2,1)S(1)} %bitcast.15, bf16[2,1024,672]{2,1,0:T(8,128)(2,1)S(1)} %copy-done.2), kind=kOutput, calls=%fused_computation.2 | convolution fusion | flops 1850591232 | bytes 6262784 | tf_op jit(solution)/shard_map/dot_general | solution.py:15
  180.8 0.0 copy-done.1
  180.8 0.6 copy.13
  181.4 0.0 copy-done
  181.4 0.6 copy.14
Async XLA Ops:
  165.5 4.4 %copy-start.2 = (bf16[2,1024,672]{2,1,0:T(8,128)(2,1)S(1)}, bf16[2,1024,672]{2,1,0:T(8,128)(2,1)}, u32[]{:S(2)}) copy-start(bf16[2,1024,672]{2,1,0:T(8,128)(2,1)} %get-tuple-element.11) | copy-start | bytes 8257540
  177.2 3.6 %copy-start.1 = (bf16[64,672]{1,0:T(8,128)(2,1)S(1)}, bf16[64,672]{1,0:T(8,128)(2,1)}, u32[]{:S(2)}) copy-start(bf16[64,672]{1,0:T(8,128)(2,1)} %get-tuple-element.21) | copy-start | bytes 258052
  177.2 4.3 %copy-start = (bf16[64,672]{1,0:T(8,128)(2,1)S(1)}, bf16[64,672]{1,0:T(8,128)(2,1)}, u32[]{:S(2)}) copy-start(bf16[64,672]{1,0:T(8,128)(2,1)} %get-tuple-element.22) | copy-start | bytes 258052

commit v3 on v2

--- a/solution.py
+++ b/solution.py
@@ -18,12 +18,12 @@
 
 
 def kernel(
-    gran_ref, x_ref, g_ref, wg_ref, wu_ref, wd_ref,
-    out_ref, dx_ref, xg_out, hid_out,
-    xg, hid, acc, keep, st_a, xa, st_b, zb, st_c, zc, st_z, za, st_x, xb,
+    gran_ref, x_ref, g_ref, wg_hbm, wu_hbm, wd_hbm,
+    out_ref, dx_ref, gate_out, up_out, down_out,
+    wg_ref, wu_ref, wd_ref, xg, hid, pool, st_a, xa, st_b, zb_flat, st_c, zc, st_z, za, st_x, xb,
     o_own, sib_st, sib_rx, st_y, y_rx, st_w, w_rx, ss, rs, loc,
 ):
-    cols = wg_ref.shape[1]
+    feat, cols = wg_ref.shape
     dp = lax.axis_index("dp")
     t = lax.axis_index("tensor")
     xl, z = dp // 4, dp % 4
@@ -61,6 +61,12 @@
 
     def r64(i, base=0):
         return pl.ds(pl.multiple_of(base + i * LEN, LEN), LEN)
+
+    loads = []
+    for i, (src, dst) in enumerate(((wg_hbm, wg_ref), (wu_hbm, wu_ref), (wd_hbm, wd_ref))):
+        load = pltpu.make_async_copy(src, dst, loc.at[i])
+        load.start()
+        loads.append(load)
 
     bar = pltpu.get_barrier_semaphore()
     peers = [x_peer, sibling, far_chip] + z_peer[1:] + y_chip[1:]
@@ -83,13 +89,6 @@
     i_y2 = {1: send(theirs, seqs(1, 1), y_chip[1]), 2: send(theirs, seqs(2, 1), y_chip[3])}
     i_y2[3] = send(theirs, seqs(3, 1), y_chip[2])
     i_s = {}
-    local_copies = []
-
-    def keep_in_hbm(src, dst):
-        copy = pltpu.make_async_copy(src, dst, loc.at[len(local_copies)])
-        copy.start()
-        local_copies.append(copy)
-
     def gather(p):
         if p == 0:
             got(i_sib, i_sib2)
@@ -97,35 +96,49 @@
             got(i_y[p], i_y2[p])
             i_s[p] = send(seqs(p, 0, 2), seqs(p, 2, 2), sibling)
             got(i_s[p])
-        keep_in_hbm(seqs(p, 0, 4), xg_out.at[:, pl.ds(p * 256, 256), :])
 
     s_a, s_b, s_c, s_z, s_x = {}, {}, {}, {}, {}
+
+    def acc(k, start, n=16):
+        return pl.ds(pl.multiple_of(k * 256 + start, 16), n)
+
+    def keep(p, k, start, n=16):
+        return pl.ds(pl.multiple_of(768 + (p * 3 + k) * 128 + start, 16), n)
+
+    def zb(p, d, k, start=0):
+        return pl.ds(p * 192 + d * 96 + k * 32 + start, 16)
 
     def products(p):
         gather(p)
+        if p == 0:
+            for load in loads:
+                load.wait()
         xs = xg[0, p * 256 : p * 256 + 256, :]
         gs = xg[1, p * 256 : p * 256 + 256, :]
-        acc[0] = jnp.dot(xs, wg_ref[...], preferred_element_type=F32)
-        acc[1] = jnp.dot(xs, wu_ref[...], preferred_element_type=F32)
-        acc[2] = jnp.dot(gs, wd_ref[...], preferred_element_type=F32)
+        pool[0:256, :] = jnp.dot(xs, wg_ref[...], preferred_element_type=F32)
+        pool[256:512, :] = jnp.dot(xs, wu_ref[...], preferred_element_type=F32)
+        pool[512:768, :] = jnp.dot(gs, wd_ref[...], preferred_element_type=F32)
         for k in range(3):
-            st_a[p, k] = acc[k, r64(1 - xl), :].astype(BF)
-        s_a[p] = send(st_a.at[p], xa.at[p], x_peer)
+            st_a[p * 192 + k * 64 : p * 192 + k * 64 + 64, :] = pool[acc(k, (1 - xl) * 64, 64), :].astype(BF)
+        s_a[p] = send(st_a.at[pl.ds(p * 192, 192), :], xa.at[pl.ds(p * 192, 192), :], x_peer)
         for k in range(3):
-            st_b[p, 0, k, 0:16, :] = acc[k, r16(zf, 128), :].astype(BF)
-            st_b[p, 0, k, 16:32, :] = acc[k, r16(zp, 192), :].astype(BF)
-            st_b[p, 1, k, 0:16, :] = acc[k, r16(zf, 192), :].astype(BF)
-            st_b[p, 1, k, 16:32, :] = acc[k, r16(zm, 128), :].astype(BF)
+            st_b[zb(p, 0, k, 0), :] = pool[acc(k, 128 + 16 * zf), :].astype(BF)
+            st_b[zb(p, 0, k, 16), :] = pool[acc(k, 192 + 16 * zp), :].astype(BF)
+            st_b[zb(p, 1, k, 0), :] = pool[acc(k, 192 + 16 * zf), :].astype(BF)
+            st_b[zb(p, 1, k, 16), :] = pool[acc(k, 128 + 16 * zm), :].astype(BF)
         s_b[p] = (
-            send(st_b.at[p, 0], zb.at[p, 0], z_peer[1]),
-            send(st_b.at[p, 1], zb.at[p, 1], z_peer[3]),
+            send(st_b.at[pl.ds(p * 192, 96), :], zb_flat.at[pl.ds(p * 192, 96), :], z_peer[1]),
+            send(st_b.at[pl.ds(p * 192 + 96, 96), :], zb_flat.at[pl.ds(p * 192 + 96, 96), :], z_peer[3]),
         )
         for k in range(3):
-            keep[p, k, 0:64, :] = acc[k, r64(xl), :]
-            keep[p, k, 64:80, :] = acc[k, r16(zp, 128), :]
-            keep[p, k, 80:96, :] = acc[k, r16(zm, 192), :]
-            keep[p, k, 96:112, :] = acc[k, r16(z, 128), :]
-            keep[p, k, 112:128, :] = acc[k, r16(z, 192), :]
+            pool[keep(p, k, 0, 64), :] = pool[acc(k, xl * 64, 64), :]
+            pool[keep(p, k, 64), :] = pool[acc(k, 128 + 16 * zp), :]
+            pool[keep(p, k, 80), :] = pool[acc(k, 192 + 16 * zm), :]
+            pool[keep(p, k, 96), :] = pool[acc(k, 128 + 16 * z), :]
+            pool[keep(p, k, 112), :] = pool[acc(k, 192 + 16 * z), :]
+
+    def from_x(p, k, zz):
+        return xa[r16(zz, (p * 3 + k) * 64), :].astype(F32)
 
     def second(p):
         sent = []
@@ -133,26 +146,26 @@
             got(s_b[p][d])
             for k in range(3):
                 st_c[p, d, k] = (
-                    keep[p, k, 64 + 16 * d : 80 + 16 * d, :] + zb[p, d, k, 0:16, :].astype(F32)
+                    pool[keep(p, k, 64 + 16 * d), :] + zb_flat[zb(p, d, k), :].astype(F32)
                 ).astype(BF)
             sent.append(send(st_c.at[p, d], zc.at[p, d], peer))
         s_c[p] = sent
         got(s_a[p])
         sent = []
         for r in (2, 1, 3):
-            zz = r16((z + r) % 4)
+            zz = (z + r) % 4
             for k in range(3):
-                st_z[p, r - 1, k] = (keep[p, k, zz, :] + xa[p, k, zz, :].astype(F32)).astype(BF)
+                st_z[p, r - 1, k] = (pool[keep(p, k, 16 * zz), :] + from_x(p, k, zz)).astype(BF)
             sent.append(send(st_z.at[p, r - 1], za.at[p, r - 1], z_peer[r]))
         s_z[p] = sent
 
     def third(p):
         got(*s_c[p])
         for k in range(3):
-            v0 = keep[p, k, 96:112, :] + zc[p, 0, k].astype(F32) + zb[p, 1, k, 16:32, :].astype(F32)
-            v1 = keep[p, k, 112:128, :] + zc[p, 1, k].astype(F32) + zb[p, 0, k, 16:32, :].astype(F32)
+            v0 = pool[keep(p, k, 96), :] + zc[p, 0, k].astype(F32) + zb_flat[zb(p, 1, k, 16), :].astype(F32)
+            v1 = pool[keep(p, k, 112), :] + zc[p, 1, k].astype(F32) + zb_flat[zb(p, 0, k, 16), :].astype(F32)
             st_x[p, k] = jnp.where(xl == 0, v1, v0).astype(BF)
-            keep[p, k, 64:80, :] = jnp.where(xl == 0, v0, v1)
+            pool[keep(p, k, 64), :] = jnp.where(xl == 0, v0, v1)
         s_x[p] = send(st_x.at[p], xb.at[p], x_peer)
 
     def activate(p, k, total):
@@ -182,24 +195,26 @@
         got(*s_z[p])
 
         def total_a(k):
-            v = keep[p, k, r16(z), :] + xa[p, k, r16(z), :].astype(F32)
+            v = pool[keep(p, k, 16 * z), :] + from_x(p, k, z)
             for r in range(3):
                 v = v + za[p, r, k].astype(F32)
             return v
 
         activate(p, 0, total_a)
         part = hid.at[:, 4 * p + xl, r16(z), :]
-        h_az[p] = [share(part, z_peer[r]) for r in (2, 1, 3)]
+        h_az[p] = {r: share(part, z_peer[r]) for r in (2, 1, 3)}
+        h_ax[p] = [share(part, x_peer)]
         got(s_x[p])
-        activate(p, 2, lambda k: keep[p, k, 64:80, :] + xb[p, k].astype(F32))
+        activate(p, 2, lambda k: pool[keep(p, k, 64), :] + xb[p, k].astype(F32))
         h_bx[p] = share(hid.at[:, 4 * p + 2 + xl, r16(z), :], x_peer)
 
     def spread(p):
         got(h_bx[p])
         part = hid.at[:, pl.ds(4 * p + 2, 2), r16(z), :]
         h_bz[p] = (share(part, z_peer[1]), share(part, z_peer[3]))
-        got(*h_az[p])
-        h_ax[p] = share(hid.at[:, 4 * p + xl], x_peer)
+        for r in (1, 3, 2):
+            got(h_az[p][r])
+            h_ax[p].append(share(hid.at[:, 4 * p + xl, r16((z + 4 - r) % 4), :], x_peer))
 
     def forward(p):
         got(h_bz[p][0])
@@ -210,16 +225,49 @@
 
     s_o, s_y = {}, {}
 
+    def output_rows(p, first, n):
+        seq = 4 * p + first // LEN
+        h, gd, ud = (hid[i, seq : seq + n // LEN].reshape(n, cols) for i in range(3))
+        o = contract(h, wd_ref[...], 1, 1)
+        return o, contract(gd, wg_ref[...], 1, 1) + contract(ud, wu_ref[...], 1, 1)
+
     def outputs(p):
-        got(h_ax[p], *h_bf[p])
-        keep_in_hbm(hid.at[:, pl.ds(4 * p, 4)], hid_out.at[:, pl.ds(4 * p, 4)])
-        h, gd, ud = (hid[i, 4 * p : 4 * p + 4].reshape(256, cols) for i in range(3))
-        o = contract(h, wd_ref[...], 1, 1)
-        d = contract(gd, wg_ref[...], 1, 1) + contract(ud, wu_ref[...], 1, 1)
-        for i, v in ((0, o), (1, d)):
+        got(*h_ax[p], *h_bf[p])
+        for i, v in enumerate(output_rows(p, 0, 256)):
             sib_st[p, i] = v[128:, :]
             o_own[p % 2, i] = v[:128, :]
         s_o[p] = send(sib_st.at[p], sib_rx.at[p], sibling)
+
+    def outputs_in_halves(p):
+        got(*h_bf[p])
+        for i, v in enumerate(output_rows(p, 128, 128)):
+            sib_st[p, i] = v
+        s_o[p] = send(sib_st.at[p], sib_rx.at[p], sibling)
+        got(*h_ax[p])
+        for i, v in enumerate(output_rows(p, 0, 128)):
+            o_own[p % 2, i] = v
+
+    grads = ((1, down_out, st_a), (0, gate_out, xa), (0, up_out, zb_flat))
+    stores = []
+
+    def weight_grads(n, p, rounds, last=False):
+        side, dst, stage = grads[n]
+        right = hid[n, 4 * p : 4 * (p + rounds)].reshape(256 * rounds, cols)
+        for i in range(0, feat, 256):
+            size = min(256, feat - i)
+            left = xg[side, 256 * p : 256 * (p + rounds), i : i + size]
+            v = contract(left, right, 0, 0)
+            at = slice(n * feat + i, n * feat + i + size)
+            if rounds == 1:
+                v = pool[at, :] + v
+            if last:
+                stage[i : i + size, :] = v.astype(BF)
+            else:
+                pool[at, :] = v
+        if last:
+            copy = pltpu.make_async_copy(stage.at[pl.ds(0, feat), :], dst, loc.at[3 + n])
+            copy.start()
+            stores.append(copy)
 
     def between_cores(p):
         got(s_o[p])
@@ -250,16 +298,22 @@
     forward(2)
     between_cores(1)
     owned(3)
-    owned(0)
     outputs(2)
     spread(3)
+    owned(0)
+    between_cores(2)
+    weight_grads(0, 1, 2)
+    forward(3)
     spread(0)
-    between_cores(2)
-    forward(3)
+    weight_grads(1, 1, 2)
+    outputs(3)
+    weight_grads(2, 1, 2)
+    between_cores(3)
     forward(0)
-    outputs(3)
-    between_cores(3)
-    outputs(0)
+    weight_grads(0, 3, 1)
+    weight_grads(1, 3, 1)
+    weight_grads(2, 3, 1)
+    outputs_in_halves(0)
     between_cores(0)
 
     got(s_y[1], s_y[2], s_y[3])
@@ -269,18 +323,42 @@
             v = v + y_rx[p, i].astype(F32)
         o_own[0, i] = v
         st_w[i] = v[LEN:, :].astype(BF)
-    got(send(st_w, w_rx, far_chip))
+    last = send(st_w, w_rx, far_chip)
+    for copy in s_a.values():
+        copy.wait_send()
+    for n in range(3):
+        weight_grads(n, 0, 1, True)
+    got(last)
     out_ref[...] = (o_own[0, 0, 0:LEN, :] + w_rx[0].astype(F32)).astype(BF)
     dx_ref[...] = (o_own[0, 1, 0:LEN, :] + w_rx[1].astype(F32)).astype(BF)
 
     for copy in sends:
-        copy.wait_send()
-    for copy in local_copies:
+        if all(copy is not early for early in s_a.values()):
+            copy.wait_send()
+    for copy in stores:
         copy.wait()
     assert len(sends) == N_SENDS
 
 
-N_SENDS = 12 + 4 * 19 + 3 + 1
+N_SENDS = 12 + 4 * 22 + 3 + 1
+
+
+def move(*refs):
+    loads, stores = refs[-2], refs[-1]
+    n = loads.shape[0]
+    reads = [
+        pltpu.make_async_copy(refs[i], refs[2 * n + i], loads.at[i]) for i in range(n)
+    ]
+    writes = [
+        pltpu.make_async_copy(refs[2 * n + i], refs[n + i], stores.at[i]) for i in range(n)
+    ]
+    for copy in reads:
+        copy.start()
+    for read, write in zip(reads, writes):
+        read.wait()
+        write.start()
+    for copy in writes:
+        copy.wait()
 
 
 def local(layer_input, gate_weight, up_weight, down_weight, granularity, out_grad):
@@ -288,25 +366,25 @@
     vm = pl.BlockSpec(memory_space=pltpu.VMEM)
     hbm = pl.BlockSpec(memory_space=pl.ANY)
     sm = pl.BlockSpec(memory_space=pltpu.SMEM)
-    out, dx, xg, hid = pl.pallas_call(
+    side = jax.ShapeDtypeStruct((LEN, feat), BF)
+    weight = jax.ShapeDtypeStruct((feat, cols), BF)
+    results = (side, side, weight, weight, weight)
+    parts = pl.pallas_call(
         kernel,
-        out_shape=(
-            jax.ShapeDtypeStruct((LEN, feat), BF),
-            jax.ShapeDtypeStruct((LEN, feat), BF),
-            jax.ShapeDtypeStruct((2, 1024, feat), BF),
-            jax.ShapeDtypeStruct((3, 16, LEN, cols), BF),
-        ),
-        in_specs=[sm] + [vm] * 5,
-        out_specs=(vm, vm, hbm, hbm),
+        out_shape=results,
+        in_specs=[sm, vm, vm, hbm, hbm, hbm],
+        out_specs=(vm, vm, hbm, hbm, hbm),
         scratch_shapes=[
+            pltpu.VMEM((feat, cols), BF),
+            pltpu.VMEM((feat, cols), BF),
+            pltpu.VMEM((feat, cols), BF),
             pltpu.VMEM((2, 1024, feat), BF),
             pltpu.VMEM((3, 16, LEN, cols), BF),
-            pltpu.VMEM((3, 256, cols), F32),
-            pltpu.VMEM((4, 3, 128, cols), F32),
-            pltpu.VMEM((4, 3, LEN, cols), BF),
-            pltpu.VMEM((4, 3, LEN, cols), BF),
-            pltpu.VMEM((4, 2, 3, 32, cols), BF),
-            pltpu.VMEM((4, 2, 3, 32, cols), BF),
+            pltpu.VMEM((768 + 4 * 3 * 128, cols), F32),
+            pltpu.VMEM((4 * 3 * LEN, cols), BF),
+            pltpu.VMEM((4 * 3 * LEN, cols), BF),
+            pltpu.VMEM((4 * 2 * 3 * 32, cols), BF),
+            pltpu.VMEM((4 * 2 * 3 * 32, cols), BF),
             pltpu.VMEM((4, 2, 3, 16, cols), BF),
             pltpu.VMEM((4, 2, 3, 16, cols), BF),
             pltpu.VMEM((4, 3, 3, 16, cols), BF),
@@ -322,18 +400,24 @@
             pltpu.VMEM((2, LEN, feat), BF),
             pltpu.SemaphoreType.DMA((N_SENDS,)),
             pltpu.SemaphoreType.DMA((N_SENDS,)),
-            pltpu.SemaphoreType.DMA((8,)),
+            pltpu.SemaphoreType.DMA((6,)),
         ],
         compiler_params=pltpu.CompilerParams(
             collective_id=0, has_side_effects=True, vmem_limit_bytes=62 << 20
         ),
-        cost_estimate=pl.CostEstimate(flops=12_000_000_000, bytes_accessed=20_000_000, transcendentals=0),
+        cost_estimate=pl.CostEstimate(flops=17_000_000_000, bytes_accessed=20_000_000, transcendentals=0),
     )(granularity, layer_input, out_grad, gate_weight, up_weight, down_weight.T)
-    hid = hid.reshape(3, 1024, cols)
-    down_grad = contract(xg[1], hid[0], 0, 0).astype(BF).T
-    gate_grad = contract(xg[0], hid[1], 0, 0).astype(BF)
-    up_grad = contract(xg[0], hid[2], 0, 0).astype(BF)
-    return out, dx, gate_grad, up_grad, down_grad
+    out, dx, gate_grad, up_grad, down_grad = pl.pallas_call(
+        move,
+        out_shape=results,
+        in_specs=[hbm] * 5,
+        out_specs=(hbm,) * 5,
+        scratch_shapes=[pltpu.VMEM(r.shape, BF) for r in results]
+        + [pltpu.SemaphoreType.DMA((5,))] * 2,
+        compiler_params=pltpu.CompilerParams(vmem_limit_bytes=62 << 20),
+        cost_estimate=pl.CostEstimate(flops=0, bytes_accessed=11_000_000, transcendentals=0),
+    )(*parts)
+    return out, dx, gate_grad, up_grad, down_grad.T
 
 
 def solution(mesh):

time: 184 us -> 171 us (0.929)
  matrix products: 10.9 us -> 0 us
  local copies, waits for them, and re-layouts: 5.7 us -> 0 us
  Pallas kernels: 165 us -> 169 us
    dot_general x3 -> x0, matrix products: 10.9 us -> none  [contract(): lax.dot_general(left, right, (((left_dim,), (right_dim,)), ((), ())), pre...]
    pallas_call x1 -> x2, Pallas kernels: 165 us -> 169 us  [the longest x1 165 us: local(): pl.pallas_call(kernel, out_shape=results, in_specs=[sm, vm, vm, hbm, hbm,...]
    slice x1 -> x0, local copies, waits for them, and re-layouts: 4.24 us -> none  [local(): down_grad = contract(xg[1], hid[0], 0, 0).astype(BF).T]
where the time goes in v3:
time: 171 us; the launch traced here: 170 us
  Pallas kernels  169 us (99%)
    pallas_call x1, Pallas kernels, local(): pl.pallas_call(kernel, out_shape=results, in_specs=[sm, vm, vm, hbm, hbm,...  165 us
    pallas_call x1, Pallas kernels, local(): pl.pallas_call(move, out_shape=results, in_specs=[hbm] * 5, out_specs=(hb...  4.68 us

profile of v3, /device:TPU:0, one launch (start us, length us, event | category | flops | bytes accessed | tf_op | source)
XLA Modules:
  0.0 170.2 jit_solution(11848854282437792542)
XLA Ops:
  0.6 164.7 %shard_map.101 = (bf16[64,672]{1,0:T(8,128)(2,1)}, bf16[64,672]{1,0:T(8,128)(2,1)}, bf16[672,1344]{1,0:T(8,128)(2,1)}, bf16[672,1344]{1,0:T(8,128)(2,1)}, bf16[672,1344]{1,0:T(8,128)(2,1)}) custom-call(s32[16]{0:T(128)} %gran_ref.1, bf16[64,672]{1,0:T(8,128)(2,1)} %x_ref.1, bf16[64,672]{1,0:T(8,128)(2,1)} %g_ref.1, bf16[672,1344]{1,0:T(8,128)(2,1)} %wg_hbm.1, ...), custom_call_target="tpu_custom_call" | custom-call | flops 16999999488 | bytes 20000000 | tf_op jit(solution)/shard_map/pallas_call | solution.py:372
  165.3 4.7 %shard_map.102 = (bf16[64,672]{1,0:T(8,128)(2,1)}, bf16[64,672]{1,0:T(8,128)(2,1)}, bf16[672,1344]{1,0:T(8,128)(2,1)}, bf16[672,1344]{1,0:T(8,128)(2,1)}, bf16[672,1344]{1,0:T(8,128)(2,1)}) custom-call(bf16[64,672]{1,0:T(8,128)(2,1)} %get-tuple-element.15.refs_0_, bf16[64,672]{1,0:T(8,128)(2,1)} %get-tuple-element.16.refs_1_, ...), custom_call_target="tpu_custom_call" | custom-call | bytes 11000000 | tf_op jit(solution)/shard_map/pallas_call | solution.py:410

commit v4 on v3

--- a/solution.py
+++ b/solution.py
@@ -20,7 +20,7 @@
 def kernel(
     gran_ref, x_ref, g_ref, wg_hbm, wu_hbm, wd_hbm,
     out_ref, dx_ref, gate_out, up_out, down_out,
-    wg_ref, wu_ref, wd_ref, xg, hid, pool, st_a, xa, st_b, zb_flat, st_c, zc, st_z, za, st_x, xb,
+    wg_ref, wu_ref, wd_ref, ends, xg, hid, pool, pool_end, stage, st_a, xa, st_b, zb, st_c, zc, st_z, za, st_x, xb,
     o_own, sib_st, sib_rx, st_y, y_rx, st_w, w_rx, ss, rs, loc,
 ):
     feat, cols = wg_ref.shape
@@ -99,73 +99,81 @@
 
     s_a, s_b, s_c, s_z, s_x = {}, {}, {}, {}, {}
 
-    def acc(k, start, n=16):
-        return pl.ds(pl.multiple_of(k * 256 + start, 16), n)
-
-    def keep(p, k, start, n=16):
-        return pl.ds(pl.multiple_of(768 + (p * 3 + k) * 128 + start, 16), n)
-
-    def zb(p, d, k, start=0):
-        return pl.ds(p * 192 + d * 96 + k * 32 + start, 16)
+    lane = lax.broadcasted_iota(jnp.int32, (1, 128), 1)
+
+    def first_half(v):
+        return jnp.where(lane < 64, v, 0.0)
+
+    def acc(start, n=16):
+        return pl.ds(pl.multiple_of(start, 16), n)
+
+    def keep(p, start, n=16):
+        return pl.ds(pl.multiple_of(256 + p * 128 + start, 16), n)
 
     def products(p):
         gather(p)
         if p == 0:
             for load in loads:
                 load.wait()
+            g_end, u_end, d_end = (
+                jnp.concatenate([w[:, MAIN:].astype(F32), jnp.zeros((feat, 64), F32)], 1)
+                for w in (wg_ref, wu_ref, wd_ref)
+            )
+            ends[0] = (g_end + pltpu.roll(u_end, 64, 1)).astype(BF)
+            ends[1] = d_end.astype(BF)
+            ends[2] = pltpu.roll(g_end, 64, 1).astype(BF)
+            ends[3] = u_end.astype(BF)
         xs = xg[0, p * 256 : p * 256 + 256, :]
         gs = xg[1, p * 256 : p * 256 + 256, :]
-        pool[0:256, :] = jnp.dot(xs, wg_ref[...], preferred_element_type=F32)
-        pool[256:512, :] = jnp.dot(xs, wu_ref[...], preferred_element_type=F32)
-        pool[512:768, :] = jnp.dot(gs, wd_ref[...], preferred_element_type=F32)
-        for k in range(3):
-            st_a[p * 192 + k * 64 : p * 192 + k * 64 + 64, :] = pool[acc(k, (1 - xl) * 64, 64), :].astype(BF)
-        s_a[p] = send(st_a.at[pl.ds(p * 192, 192), :], xa.at[pl.ds(p * 192, 192), :], x_peer)
-        for k in range(3):
-            st_b[zb(p, 0, k, 0), :] = pool[acc(k, 128 + 16 * zf), :].astype(BF)
-            st_b[zb(p, 0, k, 16), :] = pool[acc(k, 192 + 16 * zp), :].astype(BF)
-            st_b[zb(p, 1, k, 0), :] = pool[acc(k, 192 + 16 * zf), :].astype(BF)
-            st_b[zb(p, 1, k, 16), :] = pool[acc(k, 128 + 16 * zm), :].astype(BF)
+        for at, left, right in (
+            (0, xs, wg_ref[:, :MAIN]),
+            (MAIN, xs, wu_ref[:, :MAIN]),
+            (2 * MAIN, gs, wd_ref[:, :MAIN]),
+            (3 * MAIN, xs, ends[0]),
+            (3 * MAIN + 128, gs, ends[1]),
+        ):
+            pool[0:256, at : at + right.shape[1]] = jnp.dot(left, right, preferred_element_type=F32)
+        st_a[p] = pool[acc((1 - xl) * 64, 64), :].astype(BF)
+        s_a[p] = send(st_a.at[p], xa.at[p], x_peer)
+        st_b[p, 0, 0:16, :] = pool[acc(128 + 16 * zf), :].astype(BF)
+        st_b[p, 0, 16:32, :] = pool[acc(192 + 16 * zp), :].astype(BF)
+        st_b[p, 1, 0:16, :] = pool[acc(192 + 16 * zf), :].astype(BF)
+        st_b[p, 1, 16:32, :] = pool[acc(128 + 16 * zm), :].astype(BF)
         s_b[p] = (
-            send(st_b.at[pl.ds(p * 192, 96), :], zb_flat.at[pl.ds(p * 192, 96), :], z_peer[1]),
-            send(st_b.at[pl.ds(p * 192 + 96, 96), :], zb_flat.at[pl.ds(p * 192 + 96, 96), :], z_peer[3]),
+            send(st_b.at[p, 0], zb.at[p, 0], z_peer[1]),
+            send(st_b.at[p, 1], zb.at[p, 1], z_peer[3]),
         )
-        for k in range(3):
-            pool[keep(p, k, 0, 64), :] = pool[acc(k, xl * 64, 64), :]
-            pool[keep(p, k, 64), :] = pool[acc(k, 128 + 16 * zp), :]
-            pool[keep(p, k, 80), :] = pool[acc(k, 192 + 16 * zm), :]
-            pool[keep(p, k, 96), :] = pool[acc(k, 128 + 16 * z), :]
-            pool[keep(p, k, 112), :] = pool[acc(k, 192 + 16 * z), :]
-
-    def from_x(p, k, zz):
-        return xa[r16(zz, (p * 3 + k) * 64), :].astype(F32)
+        pool[keep(p, 0, 64), :] = pool[acc(xl * 64, 64), :]
+        pool[keep(p, 64), :] = pool[acc(128 + 16 * zp), :]
+        pool[keep(p, 80), :] = pool[acc(192 + 16 * zm), :]
+        pool[keep(p, 96), :] = pool[acc(128 + 16 * z), :]
+        pool[keep(p, 112), :] = pool[acc(192 + 16 * z), :]
 
     def second(p):
         sent = []
         for d, peer in ((0, z_peer[1]), (1, z_peer[3])):
             got(s_b[p][d])
-            for k in range(3):
-                st_c[p, d, k] = (
-                    pool[keep(p, k, 64 + 16 * d), :] + zb_flat[zb(p, d, k), :].astype(F32)
-                ).astype(BF)
+            st_c[p, d] = (
+                pool[keep(p, 64 + 16 * d), :] + zb[p, d, 0:16, :].astype(F32)
+            ).astype(BF)
             sent.append(send(st_c.at[p, d], zc.at[p, d], peer))
         s_c[p] = sent
         got(s_a[p])
         sent = []
         for r in (2, 1, 3):
             zz = (z + r) % 4
-            for k in range(3):
-                st_z[p, r - 1, k] = (pool[keep(p, k, 16 * zz), :] + from_x(p, k, zz)).astype(BF)
+            st_z[p, r - 1] = (
+                pool[keep(p, 16 * zz), :] + xa[p, r16(zz), :].astype(F32)
+            ).astype(BF)
             sent.append(send(st_z.at[p, r - 1], za.at[p, r - 1], z_peer[r]))
         s_z[p] = sent
 
     def third(p):
         got(*s_c[p])
-        for k in range(3):
-            v0 = pool[keep(p, k, 96), :] + zc[p, 0, k].astype(F32) + zb_flat[zb(p, 1, k, 16), :].astype(F32)
-            v1 = pool[keep(p, k, 112), :] + zc[p, 1, k].astype(F32) + zb_flat[zb(p, 0, k, 16), :].astype(F32)
-            st_x[p, k] = jnp.where(xl == 0, v1, v0).astype(BF)
-            pool[keep(p, k, 64), :] = jnp.where(xl == 0, v0, v1)
+        v0 = pool[keep(p, 96), :] + zc[p, 0].astype(F32) + zb[p, 1, 16:32, :].astype(F32)
+        v1 = pool[keep(p, 112), :] + zc[p, 1].astype(F32) + zb[p, 0, 16:32, :].astype(F32)
+        st_x[p] = jnp.where(xl == 0, v1, v0).astype(BF)
+        pool[keep(p, 64), :] = jnp.where(xl == 0, v0, v1)
         s_x[p] = send(st_x.at[p], xb.at[p], x_peer)
 
     def activate(p, k, total):
@@ -174,17 +182,26 @@
         width = jnp.where(
             level == 0, 2688, jnp.where(level == 1, 5376, jnp.where(level == 2, 10752, 21504))
         )
-        col = t * cols + lax.broadcasted_iota(jnp.int32, (1, cols), 1)
-        mask = jnp.where(col < width, 1.0, 0.0).astype(F32)
-        gate_pre, up_pre, hidden_grad = total(0), total(1), total(2)
-        sig = jax.nn.sigmoid(gate_pre)
-        act = gate_pre * sig
+
+        def pointwise(gate_pre, up_pre, hidden_grad, first_col):
+            n = gate_pre.shape[1]
+            col = t * cols + first_col + lax.broadcasted_iota(jnp.int32, (1, n), 1)
+            mask = jnp.where(col < width, 1.0, 0.0).astype(F32)
+            sig = jax.nn.sigmoid(gate_pre)
+            act = gate_pre * sig
+            gate_delta = hidden_grad * up_pre * sig * (1.0 + gate_pre * (1.0 - sig)) * mask
+            return act * up_pre * mask, gate_delta, hidden_grad * act * mask
+
         at = 4 * p + k + xl
-        hid[0, at, r16(z), :] = (act * up_pre * mask).astype(BF)
-        hid[1, at, r16(z), :] = (
-            hidden_grad * up_pre * sig * (1.0 + gate_pre * (1.0 - sig)) * mask
-        ).astype(BF)
-        hid[2, at, r16(z), :] = (hidden_grad * act * mask).astype(BF)
+        main = pointwise(total(0, MAIN), total(MAIN, MAIN), total(2 * MAIN, MAIN), 0)
+        for i, v in enumerate(main):
+            hid[at, r16(z), i * MAIN : (i + 1) * MAIN] = v.astype(BF)
+        both = total(3 * MAIN, 128)
+        gate_end, up_end = first_half(both), first_half(pltpu.roll(both, 64, 1))
+        h, gd, ud = pointwise(gate_end, up_end, total(3 * MAIN + 128, 128), MAIN)
+        end = first_half(h) + pltpu.roll(first_half(gd), 64, 1)
+        hid[at, r16(z), 3 * MAIN : 3 * MAIN + 128] = end.astype(BF)
+        hid[at, r16(z), 3 * MAIN + 128 :] = first_half(ud).astype(BF)
 
     h_az, h_ax, h_bx, h_bz, h_bf = {}, {}, {}, {}, {}
 
@@ -194,42 +211,51 @@
     def owned(p):
         got(*s_z[p])
 
-        def total_a(k):
-            v = pool[keep(p, k, 16 * z), :] + from_x(p, k, z)
+        def total_a(at, n):
+            v = pool[keep(p, 16 * z), at : at + n] + xa[p, r16(z), at : at + n].astype(F32)
             for r in range(3):
-                v = v + za[p, r, k].astype(F32)
+                v = v + za[p, r, :, at : at + n].astype(F32)
             return v
 
+        def total_b(at, n):
+            return pool[keep(p, 64), at : at + n] + xb[p, :, at : at + n].astype(F32)
+
         activate(p, 0, total_a)
-        part = hid.at[:, 4 * p + xl, r16(z), :]
+        part = hid.at[4 * p + xl, r16(z), :]
         h_az[p] = {r: share(part, z_peer[r]) for r in (2, 1, 3)}
         h_ax[p] = [share(part, x_peer)]
         got(s_x[p])
-        activate(p, 2, lambda k: pool[keep(p, k, 64), :] + xb[p, k].astype(F32))
-        h_bx[p] = share(hid.at[:, 4 * p + 2 + xl, r16(z), :], x_peer)
+        activate(p, 2, total_b)
+        h_bx[p] = share(hid.at[4 * p + 2 + xl, r16(z), :], x_peer)
 
     def spread(p):
         got(h_bx[p])
-        part = hid.at[:, pl.ds(4 * p + 2, 2), r16(z), :]
+        part = hid.at[pl.ds(4 * p + 2, 2), r16(z), :]
         h_bz[p] = (share(part, z_peer[1]), share(part, z_peer[3]))
         for r in (1, 3, 2):
             got(h_az[p][r])
-            h_ax[p].append(share(hid.at[:, 4 * p + xl, r16((z + 4 - r) % 4), :], x_peer))
+            h_ax[p].append(share(hid.at[4 * p + xl, r16((z + 4 - r) % 4), :], x_peer))
 
     def forward(p):
         got(h_bz[p][0])
-        one = share(hid.at[:, 4 * p + 2, r16(zm), :], z_peer[1])
+        one = share(hid.at[4 * p + 2, r16(zm), :], z_peer[1])
         got(h_bz[p][1])
-        two = share(hid.at[:, 4 * p + 3, r16(zp), :], z_peer[3])
+        two = share(hid.at[4 * p + 3, r16(zp), :], z_peer[3])
         h_bf[p] = (one, two)
 
     s_o, s_y = {}, {}
 
     def output_rows(p, first, n):
         seq = 4 * p + first // LEN
-        h, gd, ud = (hid[i, seq : seq + n // LEN].reshape(n, cols) for i in range(3))
-        o = contract(h, wd_ref[...], 1, 1)
-        return o, contract(gd, wg_ref[...], 1, 1) + contract(ud, wu_ref[...], 1, 1)
+
+        def part(at, size=MAIN):
+            return hid[seq : seq + n // LEN, :, at : at + size].reshape(n, size)
+
+        o = contract(part(0), wd_ref[:, :MAIN], 1, 1) + contract(part(3 * MAIN, 128), ends[1], 1, 1)
+        d = contract(part(MAIN), wg_ref[:, :MAIN], 1, 1)
+        d = d + contract(part(2 * MAIN), wu_ref[:, :MAIN], 1, 1)
+        d = d + contract(part(3 * MAIN, 128), ends[2], 1, 1)
+        return o, d + contract(part(3 * MAIN + 128, 128), ends[3], 1, 1)
 
     def outputs(p):
         got(*h_ax[p], *h_bf[p])
@@ -247,27 +273,37 @@
         for i, v in enumerate(output_rows(p, 0, 128)):
             o_own[p % 2, i] = v
 
-    grads = ((1, down_out, st_a), (0, gate_out, xa), (0, up_out, zb_flat))
+    grads = (
+        ((1, 0, MAIN, pool), (1, 3 * MAIN, 128, pool_end)),
+        ((0, MAIN, MAIN, pool),),
+        ((0, 2 * MAIN, MAIN, pool), (0, 3 * MAIN, 256, pool)),
+    )
     stores = []
 
-    def weight_grads(n, p, rounds, last=False):
-        side, dst, stage = grads[n]
-        right = hid[n, 4 * p : 4 * (p + rounds)].reshape(256 * rounds, cols)
-        for i in range(0, feat, 256):
-            size = min(256, feat - i)
-            left = xg[side, 256 * p : 256 * (p + rounds), i : i + size]
-            v = contract(left, right, 0, 0)
-            at = slice(n * feat + i, n * feat + i + size)
-            if rounds == 1:
-                v = pool[at, :] + v
-            if last:
-                stage[i : i + size, :] = v.astype(BF)
-            else:
-                pool[at, :] = v
-        if last:
-            copy = pltpu.make_async_copy(stage.at[pl.ds(0, feat), :], dst, loc.at[3 + n])
-            copy.start()
-            stores.append(copy)
+    def weight_grads(n, p, rounds):
+        for side, at, size, total in grads[n]:
+            right = hid[4 * p : 4 * (p + rounds), :, at : at + size].reshape(256 * rounds, size)
+            where = 0 if total is pool_end else at
+            for i in range(0, feat, 256):
+                rows = slice(i, min(i + 256, feat))
+                left = xg[side, 256 * p : 256 * (p + rounds), rows]
+                v = contract(left, right, 0, 0)
+                if rounds == 1:
+                    v = total[rows, where : where + size] + v
+                total[rows, where : where + size] = v
+
+    def finish_grads(n, dst):
+        stage[n, :, 0:MAIN] = pool[0:feat, n * MAIN : (n + 1) * MAIN].astype(BF)
+        if n == 0:
+            end = pool_end[...]
+        elif n == 1:
+            end = pltpu.roll(pool[0:feat, 3 * MAIN : 3 * MAIN + 128], 64, 1)
+        else:
+            end = pool[0:feat, 3 * MAIN + 128 :]
+        stage[n, :, MAIN:] = end[:, 0:64].astype(BF)
+        copy = pltpu.make_async_copy(stage.at[n], dst, loc.at[3 + n])
+        copy.start()
+        stores.append(copy)
 
     def between_cores(p):
         got(s_o[p])
@@ -324,22 +360,22 @@
         o_own[0, i] = v
         st_w[i] = v[LEN:, :].astype(BF)
     last = send(st_w, w_rx, far_chip)
-    for copy in s_a.values():
-        copy.wait_send()
-    for n in range(3):
-        weight_grads(n, 0, 1, True)
+    for n, dst in ((0, down_out), (2, up_out), (1, gate_out)):
+        weight_grads(n, 0, 1)
+        finish_grads(n, dst)
     got(last)
     out_ref[...] = (o_own[0, 0, 0:LEN, :] + w_rx[0].astype(F32)).astype(BF)
     dx_ref[...] = (o_own[0, 1, 0:LEN, :] + w_rx[1].astype(F32)).astype(BF)
 
     for copy in sends:
-        if all(copy is not early for early in s_a.values()):
-            copy.wait_send()
+        copy.wait_send()
     for copy in stores:
         copy.wait()
     assert len(sends) == N_SENDS
 
 
+MAIN = 1280
+WIDE = 4096
 N_SENDS = 12 + 4 * 22 + 3 + 1
 
 
@@ -378,19 +414,22 @@
             pltpu.VMEM((feat, cols), BF),
             pltpu.VMEM((feat, cols), BF),
             pltpu.VMEM((feat, cols), BF),
+            pltpu.VMEM((4, feat, 128), BF),
             pltpu.VMEM((2, 1024, feat), BF),
-            pltpu.VMEM((3, 16, LEN, cols), BF),
-            pltpu.VMEM((768 + 4 * 3 * 128, cols), F32),
-            pltpu.VMEM((4 * 3 * LEN, cols), BF),
-            pltpu.VMEM((4 * 3 * LEN, cols), BF),
-            pltpu.VMEM((4 * 2 * 3 * 32, cols), BF),
-            pltpu.VMEM((4 * 2 * 3 * 32, cols), BF),
-            pltpu.VMEM((4, 2, 3, 16, cols), BF),
-            pltpu.VMEM((4, 2, 3, 16, cols), BF),
-            pltpu.VMEM((4, 3, 3, 16, cols), BF),
-            pltpu.VMEM((4, 3, 3, 16, cols), BF),
-            pltpu.VMEM((4, 3, 16, cols), BF),
-            pltpu.VMEM((4, 3, 16, cols), BF),
+            pltpu.VMEM((16, LEN, WIDE), BF),
+            pltpu.VMEM((256 + 4 * 128, WIDE), F32),
+            pltpu.VMEM((feat, 128), F32),
+            pltpu.VMEM((3, feat, cols), BF),
+            pltpu.VMEM((4, LEN, WIDE), BF),
+            pltpu.VMEM((4, LEN, WIDE), BF),
+            pltpu.VMEM((4, 2, 32, WIDE), BF),
+            pltpu.VMEM((4, 2, 32, WIDE), BF),
+            pltpu.VMEM((4, 2, 16, WIDE), BF),
+            pltpu.VMEM((4, 2, 16, WIDE), BF),
+            pltpu.VMEM((4, 3, 16, WIDE), BF),
+            pltpu.VMEM((4, 3, 16, WIDE), BF),
+            pltpu.VMEM((4, 16, WIDE), BF),
+            pltpu.VMEM((4, 16, WIDE), BF),
             pltpu.VMEM((2, 2, 128, feat), F32),
             pltpu.VMEM((4, 2, 128, feat), F32),
             pltpu.VMEM((4, 2, 128, feat), F32),

time: 171 us -> 168 us (0.982)
  Pallas kernels: 169 us -> 167 us
    pallas_call x1, Pallas kernels: 165 us -> 162 us  [local(): pl.pallas_call(kernel, out_shape=results, in_specs=[sm, vm, vm, hbm, hbm,...]
where the time goes in v4:
time: 168 us
  Pallas kernels  167 us (99%)
    pallas_call x1, Pallas kernels, local(): pl.pallas_call(kernel, out_shape=results, in_specs=[sm, vm, vm, hbm, hbm,...  162 us
    pallas_call x1, Pallas kernels, local(): pl.pallas_call(move, out_shape=results, in_specs=[hbm] * 5, out_specs=(hb...  4.68 us

profile of v4, /device:TPU:0, one launch (start us, length us, event | category | flops | bytes accessed | tf_op | source)
XLA Modules:
  0.0 167.8 jit_solution(16965438107985477237)
XLA Ops:
  0.6 162.3 %shard_map.101 = (bf16[64,672]{1,0:T(8,128)(2,1)}, bf16[64,672]{1,0:T(8,128)(2,1)}, bf16[672,1344]{1,0:T(8,128)(2,1)}, bf16[672,1344]{1,0:T(8,128)(2,1)}, bf16[672,1344]{1,0:T(8,128)(2,1)}) custom-call(s32[16]{0:T(128)} %gran_ref.1, bf16[64,672]{1,0:T(8,128)(2,1)} %x_ref.1, bf16[64,672]{1,0:T(8,128)(2,1)} %g_ref.1, bf16[672,1344]{1,0:T(8,128)(2,1)} %wg_hbm.1, ...), custom_call_target="tpu_custom_call" | custom-call | flops 16999999488 | bytes 20000000 | tf_op jit(solution)/shard_map/pallas_call | solution.py:408
  162.9 4.7 %shard_map.102 = (bf16[64,672]{1,0:T(8,128)(2,1)}, bf16[64,672]{1,0:T(8,128)(2,1)}, bf16[672,1344]{1,0:T(8,128)(2,1)}, bf16[672,1344]{1,0:T(8,128)(2,1)}, bf16[672,1344]{1,0:T(8,128)(2,1)}) custom-call(bf16[64,672]{1,0:T(8,128)(2,1)} %get-tuple-element.15.refs_0_, bf16[64,672]{1,0:T(8,128)(2,1)} %get-tuple-element.16.refs_1_, ...), custom_call_target="tpu_custom_call" | custom-call | bytes 11000000 | tf_op jit(solution)/shard_map/pallas_call | solution.py:449

commit v5 on v4

--- a/solution.py
+++ b/solution.py
@@ -110,19 +110,20 @@
     def keep(p, start, n=16):
         return pl.ds(pl.multiple_of(256 + p * 128 + start, 16), n)
 
+    def make_ends():
+        for load in loads:
+            load.wait()
+        g_end, u_end, d_end = (
+            jnp.concatenate([w[:, MAIN:].astype(F32), jnp.zeros((feat, 64), F32)], 1)
+            for w in (wg_ref, wu_ref, wd_ref)
+        )
+        ends[0] = (g_end + pltpu.roll(u_end, 64, 1)).astype(BF)
+        ends[1] = d_end.astype(BF)
+        ends[2] = pltpu.roll(g_end, 64, 1).astype(BF)
+        ends[3] = u_end.astype(BF)
+
     def products(p):
         gather(p)
-        if p == 0:
-            for load in loads:
-                load.wait()
-            g_end, u_end, d_end = (
-                jnp.concatenate([w[:, MAIN:].astype(F32), jnp.zeros((feat, 64), F32)], 1)
-                for w in (wg_ref, wu_ref, wd_ref)
-            )
-            ends[0] = (g_end + pltpu.roll(u_end, 64, 1)).astype(BF)
-            ends[1] = d_end.astype(BF)
-            ends[2] = pltpu.roll(g_end, 64, 1).astype(BF)
-            ends[3] = u_end.astype(BF)
         xs = xg[0, p * 256 : p * 256 + 256, :]
         gs = xg[1, p * 256 : p * 256 + 256, :]
         for at, left, right in (
@@ -280,7 +281,7 @@
     )
     stores = []
 
-    def weight_grads(n, p, rounds):
+    def weight_grads(n, p, rounds, last=False):
         for side, at, size, total in grads[n]:
             right = hid[4 * p : 4 * (p + rounds), :, at : at + size].reshape(256 * rounds, size)
             where = 0 if total is pool_end else at
@@ -290,10 +291,13 @@
                 v = contract(left, right, 0, 0)
                 if rounds == 1:
                     v = total[rows, where : where + size] + v
-                total[rows, where : where + size] = v
+                if last and size == MAIN:
+                    stage[n, rows, 0:MAIN] = v.astype(BF)
+                else:
+                    total[rows, where : where + size] = v
 
     def finish_grads(n, dst):
-        stage[n, :, 0:MAIN] = pool[0:feat, n * MAIN : (n + 1) * MAIN].astype(BF)
+        weight_grads(n, 0, 1, True)
         if n == 0:
             end = pool_end[...]
         elif n == 1:
@@ -313,6 +317,7 @@
             st_y[p - 1] = (o_own[p % 2] + sib_rx[p]).astype(BF)
             s_y[p] = send(st_y.at[p - 1], y_rx.at[p - 1], y_chip[y_of[p]])
 
+    make_ends()
     products(0)
     products(1)
     second(0)
@@ -361,7 +366,6 @@
         st_w[i] = v[LEN:, :].astype(BF)
     last = send(st_w, w_rx, far_chip)
     for n, dst in ((0, down_out), (2, up_out), (1, gate_out)):
-        weight_grads(n, 0, 1)
         finish_grads(n, dst)
     got(last)
     out_ref[...] = (o_own[0, 0, 0:LEN, :] + w_rx[0].astype(F32)).astype(BF)

time: 168 us -> 168 us (level)
  no operation moved by 1% of the time
where the time goes in v5:
time: 168 us
  Pallas kernels  167 us (99%)
    pallas_call x1, Pallas kernels, local(): pl.pallas_call(kernel, out_shape=results, in_specs=[sm, vm, vm, hbm, hbm,...  162 us
    pallas_call x1, Pallas kernels, local(): pl.pallas_call(move, out_shape=results, in_specs=[hbm] * 5, out_specs=(hb...  4.68 us

profile of v5, /device:TPU:0, one launch (start us, length us, event | category | flops | bytes accessed | tf_op | source)
XLA Modules:
  0.0 167.8 jit_solution(12893399730125259775)
XLA Ops:
  0.6 162.3 %shard_map.101 = (bf16[64,672]{1,0:T(8,128)(2,1)}, bf16[64,672]{1,0:T(8,128)(2,1)}, bf16[672,1344]{1,0:T(8,128)(2,1)}, bf16[672,1344]{1,0:T(8,128)(2,1)}, bf16[672,1344]{1,0:T(8,128)(2,1)}) custom-call(s32[16]{0:T(128)} %gran_ref.1, bf16[64,672]{1,0:T(8,128)(2,1)} %x_ref.1, bf16[64,672]{1,0:T(8,128)(2,1)} %g_ref.1, bf16[672,1344]{1,0:T(8,128)(2,1)} %wg_hbm.1, ...), custom_call_target="tpu_custom_call" | custom-call | flops 16999999488 | bytes 20000000 | tf_op jit(solution)/shard_map/pallas_call | solution.py:412
  162.9 4.7 %shard_map.102 = (bf16[64,672]{1,0:T(8,128)(2,1)}, bf16[64,672]{1,0:T(8,128)(2,1)}, bf16[672,1344]{1,0:T(8,128)(2,1)}, bf16[672,1344]{1,0:T(8,128)(2,1)}, bf16[672,1344]{1,0:T(8,128)(2,1)}) custom-call(bf16[64,672]{1,0:T(8,128)(2,1)} %get-tuple-element.15.refs_0_, bf16[64,672]{1,0:T(8,128)(2,1)} %get-tuple-element.16.refs_1_, ...), custom_call_target="tpu_custom_call" | custom-call | bytes 11000000 | tf_op jit(solution)/shard_map/pallas_call | solution.py:453
